TPU v7x, 32 devices: a whole 2x2x4 slice. The times are simulated.
32 devices in a mesh: slab: 8 (over z, y), grp: 4 (over x, core).
Axes of the slice: x: 2, y: 2, z: 4, core: 2. Of those that a mesh axis runs over, the one named last changes fastest.
Arguments:
- pencils: float32 [256, 256, 512], P('slab', 'grp'), may hold values from -6 to 6
- send_map: int32 [8, 4, 8, 16], P('slab', 'grp'), may hold values from -1 to 8191, as said below
- interp_index: int32 [2, 8, 8, 256], P(None, 'slab', None, 'grp'), may hold values from 0 to 127, as said below
- interp_frac: float32 [8, 8, 256], P('slab', None, 'grp'), may hold values from 0 to 1
- ori_count: int32 [8], P('slab'), may hold values from 1 to 8, as said below
- spectra: bfloat16 [64, 256, 512], P('slab', 'grp'), may hold values from -6 to 6
- class_ids: int32 [64], P('slab'), may hold values from 0 to 15
- ctf_table: bfloat16 [16, 256, 256], P(None, 'grp'), may hold values from -1 to 1
Outputs:
- scores: float32 [64, 512], P('slab', 'grp')
Inputs may be any that keep to these rules, and one draw needn't show every extreme that they name: `send_map`: slots with index 16 or more are never used; for every row group and owner, the used slots of one source come first, at least one, and one source fills all 16. `interp_index`: every entry names a slot that send_map fills for that owner and row group. `ori_count`: some owner lists 8 orientations.
All inputs are finite; a program needn't handle non-finite values.
Results may differ from a plain program's by a relative error of at most 0.005.
Values may be sent and summed in bfloat16 or wider, within the bound.
A program may use at most 64 MiB of HBM per device.

v0:
```python
import math

import jax
import jax.numpy as jnp
from jax import lax
from jax.sharding import PartitionSpec as P

NF = 256
CAP = 16
ORI_MAX = 8
TSIDE = 8
CLASSES = 16
PART_DEV = 8
TRANS = 64


def phase_factors(first_row, row_total):
    side_ids = jnp.arange(TSIDE, dtype=jnp.int32) - TSIDE // 2
    rows_u = first_row + jnp.arange(row_total, dtype=jnp.int32)
    cols_v = jnp.arange(NF, dtype=jnp.int32)
    turns_u = side_ids[:, None] * rows_u[None, :] % NF
    turns_v = side_ids[:, None] * cols_v[None, :] % NF
    angle_u = -2.0 * math.pi / NF * turns_u.astype(jnp.float32)
    angle_v = -2.0 * math.pi / NF * turns_v.astype(jnp.float32)
    return (jnp.cos(angle_u), jnp.sin(angle_u), jnp.cos(angle_v), jnp.sin(angle_v))


def shift_score(slice_rows, weighted, factors):
    cos_u, sin_u, cos_v, sin_v = factors
    row_total = slice_rows.shape[0]
    cu = cos_u[:, None, :, None]
    su = sin_u[:, None, :, None]
    cv = cos_v[None, :, None, :]
    sv = sin_v[None, :, None, :]
    cosines = (cu * cv - su * sv).reshape(TRANS, row_total, NF)
    sines = (su * cv + cu * sv).reshape(TRANS, row_total, NF)
    real_part = slice_rows[None, :, :NF]
    imag_part = slice_rows[None, :, NF:]
    shifted = jnp.concatenate(
        [real_part * cosines - imag_part * sines, real_part * sines + imag_part * cosines], axis=-1
    ).astype(jnp.bfloat16)
    flat_refs = shifted.reshape(TRANS, -1)
    return (
        lax.dot_general(
            weighted, flat_refs, (((1,), (1,)), ((), ())), preferred_element_type=jnp.float32
        )
        / NF
    )


def shards(pencils, send_map, interp_index, interp_frac, ori_count, spectra, class_ids, ctf_table):
    slab_depth = NF // lax.axis_size("slab")
    freq_index = jnp.arange(NF, dtype=jnp.int32)
    phase_turns = freq_index[:, None] * freq_index[None, :] % NF
    angles = 2.0 * math.pi / NF * phase_turns.astype(jnp.float32)
    cosine = jnp.cos(angles)
    sine_table = jnp.sin(angles)
    norm_scale = 1.0 / math.sqrt(NF)
    real_in = pencils[..., :NF]
    imag_in = pencils[..., NF:]
    highest = lax.Precision.HIGHEST
    real_out = (
        jnp.einsum("yxz,zk->kyx", real_in, cosine, precision=highest)
        + jnp.einsum("yxz,zk->kyx", imag_in, sine_table, precision=highest)
    ) * norm_scale
    imag_out = (
        jnp.einsum("yxz,zk->kyx", imag_in, cosine, precision=highest)
        - jnp.einsum("yxz,zk->kyx", real_in, sine_table, precision=highest)
    ) * norm_scale
    planes = jnp.stack([real_out, imag_out], axis=2).astype(jnp.bfloat16)
    slab_planes = lax.all_to_all(planes, "slab", split_axis=0, concat_axis=1, tiled=True)
    gathered = lax.all_gather(slab_planes, "grp", axis=3, tiled=True)
    row_table = gathered.reshape(slab_depth * NF, 2 * NF)
    slot_map = send_map[0, 0]
    picked = jnp.take(row_table, jnp.maximum(slot_map, 0).reshape(-1), axis=0)
    picked = picked * (slot_map >= 0).reshape(-1, 1).astype(jnp.bfloat16)
    outgoing = picked.reshape(slot_map.shape[0], CAP, 2 * NF)
    arrived = lax.all_to_all(outgoing, "slab", split_axis=0, concat_axis=0, tiled=True)
    buffer = arrived.reshape(-1, 2 * NF)
    rows_local = interp_frac.shape[2]
    tap_index = interp_index[:, 0]
    weights_tap = interp_frac[0][..., None]
    lower_rows = jnp.take(buffer, tap_index[0].reshape(-1), axis=0).reshape(
        ORI_MAX, rows_local, 2 * NF
    )
    upper_rows = jnp.take(buffer, tap_index[1].reshape(-1), axis=0).reshape(
        ORI_MAX, rows_local, 2 * NF
    )
    slices = (1.0 - weights_tap) * lower_rows.astype(jnp.float32) + weights_tap * upper_rows.astype(
        jnp.float32
    )
    onehot = (class_ids[:, None] == jnp.arange(CLASSES, dtype=jnp.int32)[None, :]).astype(
        jnp.bfloat16
    )
    ctf_rows = jnp.dot(
        onehot, ctf_table.reshape(CLASSES, -1), preferred_element_type=jnp.float32
    ).reshape(PART_DEV, rows_local, NF)
    weighted = (
        (jnp.concatenate([ctf_rows, ctf_rows], axis=-1) * spectra.astype(jnp.float32))
        .astype(jnp.bfloat16)
        .reshape(PART_DEV, -1)
    )
    first_row = lax.axis_index("grp") * rows_local
    factors = phase_factors(first_row, rows_local)
    live_count = ori_count[0]

    def orient_score(orient):
        result = shift_score(slices[orient], weighted, factors)
        return jnp.where(orient < live_count, result, jnp.zeros_like(result))

    blocks_out = lax.map(orient_score, jnp.arange(ORI_MAX, dtype=jnp.int32))
    partial_scores = jnp.transpose(blocks_out, (1, 0, 2)).reshape(PART_DEV, ORI_MAX * TRANS)
    return lax.psum_scatter(partial_scores, "grp", scatter_dimension=1, tiled=True)


def solution(mesh):
    return jax.shard_map(
        shards,
        mesh=mesh,
        in_specs=(
            P("slab", "grp", None),
            P("slab", "grp", None, None),
            P(None, "slab", None, "grp"),
            P("slab", None, "grp"),
            P("slab"),
            P("slab", "grp", None),
            P("slab"),
            P(None, "grp", None),
        ),
        out_specs=P("slab", "grp"),
        check_vma=False,
    )
```

profile of v0, /device:TPU:1, one launch (start us, length us, event | category | flops | bytes accessed | tf_op | source)
XLA Modules:
  0.0 353.7 jit_solution(2687098208419583319)
XLA Ops:
  6.5 4.6 %fusion.26 = f32[256,32,64]{0,2,1:T(8,128)S(1)} fusion(f32[32,64,512]{2,1,0:T(8,128)} %param.12), kind=kOutput, calls=%fused_computation.47 | convolution fusion | flops 1611530240 | bytes 4194304 | tf_op jit(solution)/shard_map/yxz,zk->kyx/dot_general | solution.py:64
  11.2 2.9 fusion.24
  14.1 2.9 fusion.36
  16.9 2.9 fusion.39
  20.1 6.8 %copy.17 = bf16[256,32,2,64]{3,1,2,0:T(8,128)(2,1)} copy(bf16[256,32,2,64]{0,3,1,2:T(8,128)(2,1)S(1)} %pad_maximum_fusion.1) | data formatting | bytes 4194304 | tf_op jit(solution)/shard_map/stack | solution.py:70
  26.9 6.4 %reshape.160 = bf16[8,2,65536]{2,1,0:T(2,128)(2,1)S(1)} reshape(bf16[256,2,32,64]{3,2,1,0:T(8,128)(2,1)} %bitcast.103) | data formatting | bytes 4194304
  33.3 53.7 %all_to_all.23 = bf16[8,2,65536]{2,1,0:T(2,128)(2,1)} all-to-all(bf16[8,2,65536]{2,1,0:T(2,128)(2,1)S(1)} %reshape.160), channel_id=1, replica_groups=mesh['slab'=8,'grp'=4] {'slab'}, dimensions={0} | all-to-all | bytes 4194304 | tf_op jit(solution)/shard_map/all_to_all | solution.py:71
  86.9 7.4 %reshape.161 = bf16[256,2,32,64]{3,2,1,0:T(8,128)(2,1)} reshape(bf16[8,2,65536]{2,1,0:T(2,128)(2,1)} %all_to_all.23) | data formatting | bytes 4194304
  94.3 5.3 %copy.18 = bf16[32,8,32,2,64]{4,2,1,3,0:T(8,128)(2,1)} copy(bf16[32,8,32,2,64]{4,2,3,0,1:T(8,128)(2,1)} %bitcast.104) | data formatting | bytes 4194304 | tf_op jit(solution)/shard_map/all_to_all | solution.py:71
  99.6 5.8 %copy.19 = bf16[32,256,2,64]{1,0,2,3:T(8,128)(2,1)} copy(bf16[32,256,2,64]{3,1,2,0:T(8,128)(2,1)} %bitcast.105) | data formatting | bytes 4194304 | tf_op jit(solution)/shard_map/all_to_all | solution.py:71
  106.7 57.9 %all-gather.2.cloned.1.call-done = bf16[32,256,2,256]{1,0,2,3:T(8,128)(2,1)} async-done(((bf16[32,256,2,64]{1,0,2,3:T(8,128)(2,1)}), bf16[32,256,2,256]{1,0,2,3:T(8,128)(2,1)}) %all-gather.2.cloned.1.call-update) | async-done | bytes 8388624 | tf_op jit(solution)/shard_map/all_gather | solution.py:72
  164.5 15.6 %copy.20 = bf16[32,256,2,256]{3,2,1,0:T(2,128)(2,1)} copy(bf16[32,256,2,256]{1,0,2,3:T(8,128)(2,1)} %all-gather.2.cloned.1.call-done) | data formatting | bytes 16777216 | tf_op jit(solution)/shard_map/all_gather | solution.py:72
  180.2 8.0 %copy.26 = bf16[1024,8,2,256]{3,1,2,0:T(8,128)(2,1)} copy(bf16[1024,8,2,256]{3,2,1,0:T(2,128)(2,1)} %bitcast.101) | data formatting | bytes 16777216
  188.2 5.3 %gather_fusion = bf16[128,512]{1,0:T(8,128)(2,1)S(1)} fusion(bf16[8192,512]{1,0:T(8,128)(2,1)} %bitcast.106, s32[1024]{0:T(1024)S(1)} %pad_clamp_fusion.2), kind=kCustom, calls=%fused_computation.2 | custom fusion | bytes 262656 | tf_op jit(solution)/shard_map/jit(_take)/gather | solution.py:75
  193.5 0.7 select_multiply_fusion
  194.3 5.2 %all-to-all-start.1 = ((bf16[8,16,512]{2,1,0:T(8,128)(2,1)}), bf16[8,16,512]{2,1,0:T(8,128)(2,1)S(1)}, u32[]{:S(2)}, u32[]{:S(2)}) async-start(bf16[8,16,512]{2,1,0:T(8,128)(2,1)} %select_multiply_fusion), calls=%async_computation.1 | async-start | bytes 262144 | tf_op jit(solution)/shard_map/all_to_all | solution.py:78
  199.6 6.1 %all-to-all-done.1 = bf16[8,16,512]{2,1,0:T(8,128)(2,1)S(1)} async-done(((bf16[8,16,512]{2,1,0:T(8,128)(2,1)}), bf16[8,16,512]{2,1,0:T(8,128)(2,1)S(1)}, u32[]{:S(2)}, u32[]{:S(2)}) %all-to-all-start.1) | async-done | bytes 131104 | tf_op jit(solution)/shard_map/all_to_all | solution.py:78
  205.7 2.0 gather_fusion.1
  207.7 2.0 gather_fusion.2
  210.3 118.6 %while.13 = (s32[]{:T(128)}, f32[8,8,64]{2,1,0:T(8,128)S(1)}, s32[8]{0:T(128)S(1)}, s32[]{:T(128)}, f32[8,64,512]{2,1,0:T(8,128)S(1)}, /*index=5*/bf16[8,32768]{...) while((s32[]{:T(128)}, f32[8,8,64]{2,1,0:T(8,128)S(1)}, ...), condition=%wide.region_1.3_spmd.clone.clone.clone, body=%wide.region_0.2_spmd.clone.clone.clone.sunk | while | flops 56659972 | bytes 26718700 | solution.py:111
  213.3 2.2 subtract_convert_fusion.2
  215.9 4.5 %copy.37 = bf16[8,8,64,512]{3,1,2,0:T(8,128)(2,1)} copy(bf16[8,8,64,512]{3,2,1,0:T(8,128)(2,1)S(1)} %bitcast.100) | data formatting | bytes 8388608 | tf_op jit(solution)/shard_map/while
  221.7 3.4 fusion.98
  225.1 0.7 dynamic_slice.17
  228.1 2.2 subtract_convert_fusion.2
  230.7 4.5 %copy.37 = bf16[8,8,64,512]{3,1,2,0:T(8,128)(2,1)} copy(bf16[8,8,64,512]{3,2,1,0:T(8,128)(2,1)S(1)} %bitcast.100) | data formatting | bytes 8388608 | tf_op jit(solution)/shard_map/while
  236.6 3.4 fusion.98
  242.9 2.2 subtract_convert_fusion.2
  245.6 4.5 %copy.37 = bf16[8,8,64,512]{3,1,2,0:T(8,128)(2,1)} copy(bf16[8,8,64,512]{3,2,1,0:T(8,128)(2,1)S(1)} %bitcast.100) | data formatting | bytes 8388608 | tf_op jit(solution)/shard_map/while
  251.4 3.4 fusion.98
  254.7 0.7 dynamic_slice.17
  257.8 2.2 subtract_convert_fusion.2
  260.4 4.5 %copy.37 = bf16[8,8,64,512]{3,1,2,0:T(8,128)(2,1)} copy(bf16[8,8,64,512]{3,2,1,0:T(8,128)(2,1)S(1)} %bitcast.100) | data formatting | bytes 8388608 | tf_op jit(solution)/shard_map/while
  266.2 3.4 fusion.98
  272.6 2.2 subtract_convert_fusion.2
  275.2 4.5 %copy.37 = bf16[8,8,64,512]{3,1,2,0:T(8,128)(2,1)} copy(bf16[8,8,64,512]{3,2,1,0:T(8,128)(2,1)S(1)} %bitcast.100) | data formatting | bytes 8388608 | tf_op jit(solution)/shard_map/while
  281.0 3.4 fusion.98
  287.4 2.2 subtract_convert_fusion.2
  290.0 4.5 %copy.37 = bf16[8,8,64,512]{3,1,2,0:T(8,128)(2,1)} copy(bf16[8,8,64,512]{3,2,1,0:T(8,128)(2,1)S(1)} %bitcast.100) | data formatting | bytes 8388608 | tf_op jit(solution)/shard_map/while
  295.8 3.4 fusion.98
  302.2 2.2 subtract_convert_fusion.2
  304.9 4.5 %copy.37 = bf16[8,8,64,512]{3,1,2,0:T(8,128)(2,1)} copy(bf16[8,8,64,512]{3,2,1,0:T(8,128)(2,1)S(1)} %bitcast.100) | data formatting | bytes 8388608 | tf_op jit(solution)/shard_map/while
  310.7 3.4 fusion.98
  317.1 2.2 subtract_convert_fusion.2
  319.7 4.5 %copy.37 = bf16[8,8,64,512]{3,1,2,0:T(8,128)(2,1)} copy(bf16[8,8,64,512]{3,2,1,0:T(8,128)(2,1)S(1)} %bitcast.100) | data formatting | bytes 8388608 | tf_op jit(solution)/shard_map/while
  325.5 3.4 fusion.98
  328.9 0.7 reshape.122
  329.6 17.2 %reduce-scatter.2.cloned.1.call-done = f32[8,128]{1,0:T(8,128)} async-done(((f32[8,512]{1,0:T(8,128)}), f32[8,128]{1,0:T(8,128)}) %reduce-scatter.2.cloned.1.call-update) | async-done | bytes 4112 | tf_op jit(solution)/shard_map/reduce_scatter | solution.py:113
  (105 shorter events, 11.3 us)
Async XLA Ops:
  6.5 158.0 %all-gather.2.cloned.1.call-start = ((), (), s32[]{:S(2)}) async-start(), calls=%async_computation.3 | async-start | bytes 10485760 | tf_op jit(solution)/shard_map/all_gather | solution.py:72
  6.5 4.7 %copy-start = (f32[32,64,512]{2,1,0:T(8,128)S(1)}, f32[32,64,512]{2,1,0:T(8,128)}, u32[]{:S(2)}) copy-start(f32[32,64,512]{2,1,0:T(8,128)} %param.12) | copy-start | bytes 12582916
  99.6 5.9 %copy-start.4 = (s32[1,1,8,16]{3,2,1,0:T(8,128)S(1)}, s32[1,1,8,16]{3,2,1,0:T(8,128)}, u32[]{:S(2)}) copy-start(s32[1,1,8,16]{3,2,1,0:T(8,128)} %param.13) | copy-start | bytes 1540
  99.6 6.0 %copy-start.5 = (s32[2,1,8,64]{3,2,1,0:T(8,128)S(1)}, s32[2,1,8,64]{3,2,1,0:T(8,128)}, u32[]{:S(2)}) copy-start(s32[2,1,8,64]{3,2,1,0:T(8,128)} %param.14) | copy-start | bytes 12292
  99.6 6.3 %copy-start.2 = (bf16[16,64,256]{2,1,0:T(8,128)(2,1)S(1)}, bf16[16,64,256]{2,1,0:T(8,128)(2,1)}, u32[]{:S(2)}) copy-start(bf16[16,64,256]{2,1,0:T(8,128)(2,1)} %param.19) | copy-start | bytes 1572868
  99.6 6.3 %copy-start.6 = (s32[8]{0:T(128)S(1)}, s32[8]{0:T(128)}, u32[]{:S(2)}) copy-start(s32[8]{0:T(128)} %param.18) | copy-start | bytes 100
  99.6 6.7 %copy-start.1 = (bf16[8,64,512]{2,1,0:T(8,128)(2,1)S(1)}, bf16[8,64,512]{2,1,0:T(8,128)(2,1)}, u32[]{:S(2)}) copy-start(bf16[8,64,512]{2,1,0:T(8,128)(2,1)} %param.17) | copy-start | bytes 1572868
  180.2 19.4 %copy-start.3 = (f32[1,8,64]{2,1,0:T(8,128)S(1)}, f32[1,8,64]{2,1,0:T(8,128)}, u32[]{:S(2)}) copy-start(f32[1,8,64]{2,1,0:T(8,128)} %param.15) | copy-start | bytes 6148
  194.3 11.4 %all-to-all-start.1 = ((bf16[8,16,512]{2,1,0:T(8,128)(2,1)}), bf16[8,16,512]{2,1,0:T(8,128)(2,1)S(1)}, u32[]{:S(2)}, u32[]{:S(2)}) async-start(bf16[8,16,512]{2,1,0:T(8,128)(2,1)} %select_multiply_fusion), calls=%async_computation.1 | async-start | bytes 262144 | tf_op jit(solution)/shard_map/all_to_all | solution.py:78
  199.5 147.3 %reduce-scatter.2.cloned.1.call-start = ((), (), s32[]{:S(2)}) async-start(), calls=%async_computation.4 | async-start | bytes 20480 | tf_op jit(solution)/shard_map/reduce_scatter | solution.py:113
Sparse Core Ops, SparseCore 0:
  105.6 58.8 all-gather.1
  329.7 17.0 reduce-scatter.1
where the time goes:
time: 356 us; the launch traced here: 354 us
  local copies, waits for them, and re-layouts  107 us (30%)
  waiting for transfers between devices  81.2 us (23%)
  blocking collectives  53.7 us (15%)
  matrix products  40.7 us (11%)
  loops' own time  27.2 us (8%)
  other arithmetic  24.7 us (7%)
  between operations  13.7 us (4%)
  starting transfers between devices  5.27 us (1%)
    all_gather x1, waiting for transfers between devices, shards(): gathered = lax.all_gather(slab_planes, 'grp', axis=3, tiled=True)  57.9 us
    all_to_all x1, blocking collectives, shards(): lax.all_to_all(planes, 'slab', split_axis=0, concat_axis=1, tiled=True)  53.7 us
    while x8, local copies, waits for them, and re-layouts  35.9 us
    another operation x1, loops' own time, shards(): blocks_out = lax.map(orient_score, jnp.arange(ORI_MAX, dtype=jnp.int32))  27.2 us
    dot_general x8, matrix products, shift_score(): lax.dot_general(weighted, flat_refs, (((1,), (1,)), ((), ())), preferred_...  27 us
    unnamed x17, local copies, waits for them, and re-layouts  21.8 us
    another operation x8, other arithmetic  17.8 us
    reduce_scatter x1, waiting for transfers between devices, shards(): lax.psum_scatter(partial_scores, 'grp', scatter_dimension=1, tiled=True)  17.2 us
  transfers between devices with their start and end apart: 3, of which 3 were waited for; matrix products, arithmetic and copies ran while one was open for 0% of the time, Pallas kernels for 0%

commit v1 on v0

--- a/solution.py
+++ b/solution.py
@@ -2,7 +2,10 @@
 
 import jax
 import jax.numpy as jnp
+import numpy as np
 from jax import lax
+from jax.experimental import pallas as pl
+from jax.experimental.pallas import tpu as pltpu
 from jax.sharding import PartitionSpec as P
 
 NF = 256
@@ -113,9 +116,331 @@
     return lax.psum_scatter(partial_scores, "grp", scatter_dimension=1, tiled=True)
 
 
+MESH = pl.DeviceIdType.MESH
+CAP_FAST = 32
+
+
+def dft_table():
+    turns = np.outer(np.arange(NF), np.arange(NF)) % NF
+    angle = 2.0 * np.pi / NF * turns
+    cos, sin = np.cos(angle) / math.sqrt(NF), np.sin(angle) / math.sqrt(NF)
+    return np.block([[cos, sin], [-sin, cos]]).astype(jnp.bfloat16)
+
+
+def column_phases():
+    side = np.arange(TSIDE) - TSIDE // 2
+    angle = 2.0 * np.pi / NF * (np.outer(np.arange(NF), side) % NF)
+    cos, sin = np.tile(np.cos(angle), (1, TSIDE)), np.tile(np.sin(angle), (1, TSIDE))
+    full = np.block([[cos, -sin], [sin, cos]]).astype(np.float32)
+    high = full.astype(jnp.bfloat16)
+    low = (full - high.astype(np.float32)).astype(jnp.bfloat16)
+    return np.concatenate([high, low], axis=1)
+
+
+def row_phases():
+    side = np.arange(TSIDE) - TSIDE // 2
+    angle = 2.0 * np.pi / NF * (np.outer(np.arange(NF), side) % NF)
+    cos, sin = np.repeat(np.cos(angle), TSIDE, 1), np.repeat(np.sin(angle), TSIDE, 1)
+    return np.concatenate([cos, sin], axis=1).astype(np.float32)
+
+
+def iota(shape, axis):
+    return lax.broadcasted_iota(jnp.int32, shape, axis)
+
+
+def fused(
+    n_slab, n_grp, cap,
+    class_ids, ori_count, send_map, index, frac, pencils, dft, spectra, ctf, phase_v, phase_u,
+    out, load_out,
+    maps, lines, table_w, planes, spec_in, ctf_in, col_ph, row_ph, rank_ref, key_ref, picked, sendbuf,
+    recv, weighted, product, part_send, part_recv,
+    load_sem, line_sem, map_send, map_recv, row_send, row_recv, sum_send, sum_recv,
+):
+    s, g = lax.axis_index("slab"), lax.axis_index("grp")
+    ky_loc, kx_loc = pencils.shape[0], pencils.shape[1]
+    rows_u = spectra.shape[1]
+    slots = n_slab * CAP
+    chunks = lines.shape[0]
+    step = ky_loc // chunks
+    peers = [(dg, ds) for dg in range(n_grp) for ds in range(n_slab) if dg + ds > 0]
+
+    def peer(dg, ds):
+        return lax.rem(s + ds, n_slab), lax.rem(g + dg, n_grp)
+
+    barrier = pltpu.get_barrier_semaphore()
+    for dg, ds in peers:
+        pl.semaphore_signal(barrier, inc=1, device_id=peer(dg, ds), device_id_type=MESH)
+    loads = [
+        pltpu.make_async_copy(a, b, load_sem.at[i])
+        for i, (a, b) in enumerate(
+            [(dft, table_w), (ctf, ctf_in), (spectra, spec_in), (phase_v, col_ph),
+             (phase_u.at[pl.ds(pl.multiple_of(g * rows_u, rows_u), rows_u)], row_ph)]
+        )
+    ]
+    line_loads = [
+        pltpu.make_async_copy(pencils.at[pl.ds(c * step, step)], lines.at[c], line_sem.at[c])
+        for c in range(chunks)
+    ]
+    loads[0].start()
+    for copy in line_loads:
+        copy.start()
+    for copy in loads[1:]:
+        copy.start()
+    own_map = send_map[...]
+    maps[s, g] = jnp.concatenate([own_map] * n_slab, axis=1)
+
+    pl.semaphore_wait(barrier, len(peers))
+
+    def map_copy(to, whose):
+        return pltpu.make_async_remote_copy(
+            src_ref=maps.at[s, g], dst_ref=maps.at[whose[0], whose[1]],
+            send_sem=map_send.at[to[0], to[1]], recv_sem=map_recv.at[whose[0], whose[1]],
+            device_id=to, device_id_type=MESH)
+
+    for dg, ds in peers:
+        map_copy(peer(dg, ds), (s, g)).start()
+
+    loads[0].wait()
+    for c in range(chunks):
+        line_loads[c].wait()
+        block = lines[c].reshape(step * kx_loc, 2 * NF).astype(jnp.bfloat16)
+        lanes = lax.dot_general(
+            table_w[...], block, (((1,), (1,)), ((), ())), preferred_element_type=jnp.float32
+        ).astype(jnp.bfloat16)
+        for h in range(step // 2):
+            planes[c * (step // 2) + h, :, :128] = lanes[:NF, h * 128:(h + 1) * 128]
+            planes[c * (step // 2) + h, :, 128:] = lanes[NF:, h * 128:(h + 1) * 128]
+
+    for dg, ds in peers:
+        whose = peer(dg, ds)
+        map_copy(whose, whose).wait_recv()
+
+    lane = iota((n_slab, slots), 1)
+    rows = jnp.concatenate(
+        [sum(jnp.where(lane // CAP == a, maps[a, b], 0) for a in range(n_slab)) for b in range(n_grp)],
+        axis=0,
+    )
+    shift = ky_loc.bit_length() - 1
+    used = rows >= 0
+    ky = rows & (NF - 1)
+    home = jnp.where(used, ky >> shift, -1)
+    tri = (iota((slots, slots), 0) < iota((slots, slots), 1)).astype(jnp.float32).astype(jnp.bfloat16)
+
+    def ranks(mask):
+        ones = jnp.where(mask, 1.0, 0.0)
+        return jnp.dot(ones.astype(jnp.bfloat16), tri, preferred_element_type=jnp.float32), ones
+
+    mine = home == s
+    rank, _ = ranks(mine)
+    rank = jnp.where(mine, rank, -1.0)
+    ky_own = ky & (ky_loc - 1)
+    kz = (iota(rows.shape, 1) // CAP) * (NF // n_slab) + (rows >> 8)
+    code = (((ky_own >> 1) * NF + kz) * 2 + (ky_own & 1) + 1).astype(jnp.float32)
+    for b in range(n_grp):
+        rank_ref[b] = rank[b * n_slab:(b + 1) * n_slab]
+        key_ref[b] = code[b * n_slab:(b + 1) * n_slab]
+    most = jnp.zeros((rows.shape[0], 1), jnp.float32)
+    for a in range(n_slab):
+        most = jnp.maximum(most, jnp.sum(jnp.where(home == a, 1.0, 0.0), axis=1, keepdims=True))
+    load_out[...] = jnp.broadcast_to(jnp.max(most, axis=0, keepdims=True), load_out.shape)
+
+    def row_copy(to, whose):
+        return pltpu.make_async_remote_copy(
+            src_ref=sendbuf.at[to[1], to[0]],
+            dst_ref=recv.at[whose[1], pl.ds(pl.multiple_of(whose[0] * cap, cap), cap)],
+            send_sem=row_send.at[to[1], to[0]], recv_sem=row_recv.at[whose[1], whose[0]],
+            device_id=to, device_id_type=MESH)
+
+    pairs = ky_loc // 2
+    at_once = 256 // cap
+    lane256 = iota((256, NF), 1)
+    lane128 = iota((256, 128), 1)
+    for dg in [1, 2, 3, 0][:n_grp]:
+        to_g = lax.rem(g + dg, n_grp)
+        for q in range(n_slab // at_once):
+            rk = rank_ref[to_g, q * at_once:(q + 1) * at_once]
+            cd = key_ref[to_g, q * at_once:(q + 1) * at_once]
+            places = iota((at_once, cap, slots), 1).astype(jnp.float32)
+            hit = jnp.where(rk[:, None, :] == places, cd[:, None, :], 0.0)
+            found = (jnp.sum(hit, axis=2, keepdims=True) - 1.0).reshape(256, 1).astype(jnp.int32)
+            odd = (found & 1) == 1
+            where_row = found >> 1
+            for j in range(pairs):
+                picked[:, j * NF:(j + 1) * NF] = jnp.where(
+                    where_row - j * NF == lane256, 1.0, 0.0).astype(jnp.bfloat16)
+            got = jnp.dot(picked[...], planes[...].reshape(pairs * NF, 256),
+                          preferred_element_type=jnp.float32)
+            a, b = got[:, :128], got[:, 128:]
+            row = jnp.where(lane128 < 64, jnp.where(odd, pltpu.roll(a, 64, 1), a),
+                            jnp.where(odd, b, pltpu.roll(b, 64, 1)))
+            sendbuf[to_g, q * at_once:(q + 1) * at_once] = row.astype(jnp.bfloat16).reshape(at_once, cap, 128)
+        for ds in range(n_slab):
+            if dg + ds > 0:
+                row_copy(peer(dg, ds), (s, g)).start()
+    recv[g, pl.ds(pl.multiple_of(s * cap, cap), cap)] = sendbuf[g, s]
+
+    for copy in loads[1:]:
+        copy.wait()
+    for p in range(PART_DEV):
+        ctf_rows = ctf_in[class_ids[p]].astype(jnp.float32)
+        for part in range(2):
+            weighted[p, :, part * NF:(part + 1) * NF] = (
+                ctf_rows * spec_in[p, :, part * NF:(part + 1) * NF].astype(jnp.float32)
+            ).astype(jnp.bfloat16)
+
+    own = jnp.sum(jnp.where(lane // CAP == iota((n_slab, slots), 0), maps_row(maps, s, g, n_slab), 0),
+                  axis=0, keepdims=True)
+    own_home = jnp.where(own >= 0, (own & (NF - 1)) >> shift, -1)
+    from_a = own_home == iota((n_slab, slots), 0)
+    own_rank, ones = ranks(from_a)
+    base = (iota((n_slab, slots), 0) * cap).astype(jnp.float32)
+    place = jnp.sum(ones * (own_rank + base + 1.0), axis=0, keepdims=True) - 1.0
+    spread = jnp.where(place == iota((n_slab * cap, slots), 0).astype(jnp.float32), 1.0, 0.0).astype(jnp.bfloat16)
+
+    for dg, ds in peers:
+        whose = peer(dg, ds)
+        row_copy(whose, whose).wait_recv()
+    lists = [
+        lax.dot_general(spread, recv[b], (((0,), (0,)), ((), ())), preferred_element_type=jnp.float32)
+        for b in range(n_grp)
+    ]
+    lane_s = iota((slots, 128), 1)
+    real, imag = [], []
+    for b in range(0, n_grp, 2):
+        x, y = lists[b], lists[b + 1]
+        real.append(jnp.where(lane_s < 64, x, pltpu.roll(y, 64, 1)))
+        imag.append(jnp.where(lane_s < 64, pltpu.roll(x, 64, 1), y))
+    received = jnp.concatenate(real + imag, axis=1).astype(jnp.bfloat16)
+    received = jnp.concatenate([received, received], axis=0)
+
+    def sum_copy(to_g, whose_g):
+        return pltpu.make_async_remote_copy(
+            src_ref=part_send.at[to_g], dst_ref=part_recv.at[whose_g],
+            send_sem=sum_send.at[to_g], recv_sem=sum_recv.at[whose_g],
+            device_id=(s, to_g), device_id_type=MESH)
+
+    slot_id = iota((slots, rows_u), 0)
+    live = ori_count[0]
+    lane_p = iota((PART_DEV, 128), 1)
+    for dg in [1, 2, 3, 0][:n_grp]:
+        to_g = lax.rem(g + dg, n_grp)
+        folded = []
+        for half in range(2):
+            o = to_g * 2 + half
+            i0 = index[0, pl.ds(o, 1), :]
+            i1 = index[1, pl.ds(o, 1), :]
+            w = frac[pl.ds(o, 1), :]
+            taps = jnp.where(slot_id == i0, 1.0 - w, 0.0) + jnp.where(slot_id == i1, w, 0.0)
+            high = taps.astype(jnp.bfloat16)
+            low = (taps - high.astype(jnp.float32)).astype(jnp.bfloat16)
+            rows_o = lax.dot_general(
+                jnp.concatenate([high, low], axis=0), received, (((0,), (0,)), ((), ())),
+                preferred_element_type=jnp.float32)
+            sr, si = rows_o[:, :NF], rows_o[:, NF:]
+            for p in range(PART_DEV):
+                wr = weighted[p, :, :NF].astype(jnp.float32)
+                wi = weighted[p, :, NF:].astype(jnp.float32)
+                product[p * rows_u:(p + 1) * rows_u, :NF] = (wr * sr + wi * si).astype(jnp.bfloat16)
+                product[p * rows_u:(p + 1) * rows_u, NF:] = (wr * si - wi * sr).astype(jnp.bfloat16)
+            z = jnp.dot(product[...], col_ph[...], preferred_element_type=jnp.float32)
+            z = (z[:, :128] + z[:, 128:]).reshape(PART_DEV, rows_u, 128)
+            t = jnp.sum(z * row_ph[...][None], axis=1)
+            t = (t + pltpu.roll(t, 64, 1)) * (1.0 / NF)
+            folded.append(jnp.where(o < live, t, 0.0))
+        block = jnp.where(lane_p < 64, folded[0], folded[1])
+        if dg > 0:
+            part_send[to_g] = block
+            sum_copy(to_g, g).start()
+        else:
+            total = block
+    for dg in range(1, n_grp):
+        from_g = lax.rem(g + dg, n_grp)
+        sum_copy(from_g, from_g).wait_recv()
+        total += part_recv[from_g]
+    out[...] = total
+
+    for dg, ds in peers:
+        to = peer(dg, ds)
+        map_copy(to, (s, g)).wait_send()
+        row_copy(to, (s, g)).wait_send()
+    for dg in range(1, n_grp):
+        sum_copy(lax.rem(g + dg, n_grp), g).wait_send()
+
+
+def maps_row(maps, s, g, n_slab):
+    return jnp.concatenate([maps[a, g, pl.ds(s, 1), :] for a in range(n_slab)], axis=0)
+
+
+def run_fused(n_slab, n_grp, cap, collective_id, args):
+    pencils, send_map, index, frac, ori_count, spectra, class_ids, ctf = args
+    ky_loc, kx_loc = pencils.shape[:2]
+    rows_u = spectra.shape[1]
+    slots = n_slab * CAP
+    chunks = ky_loc // 4
+    vmem, smem, hbm = (pl.BlockSpec(memory_space=m) for m in (pltpu.VMEM, pltpu.SMEM, pl.ANY))
+    dma = pltpu.SemaphoreType.DMA
+    return pl.pallas_call(
+        lambda *refs: fused(n_slab, n_grp, cap, *refs),
+        out_shape=[
+            jax.ShapeDtypeStruct((PART_DEV, ORI_MAX * TRANS // n_grp), jnp.float32),
+            jax.ShapeDtypeStruct((8, 128), jnp.float32),
+        ],
+        in_specs=[smem, smem, vmem, vmem, vmem, hbm, hbm, hbm, hbm, hbm, hbm],
+        out_specs=[vmem, vmem],
+        scratch_shapes=[
+            pltpu.VMEM((n_slab, n_grp, n_slab, slots), jnp.int32),
+            pltpu.VMEM((chunks, 4, kx_loc, 2 * NF), jnp.float32),
+            pltpu.VMEM((2 * NF, 2 * NF), jnp.bfloat16),
+            pltpu.VMEM((ky_loc // 2, NF, 256), jnp.bfloat16),
+            pltpu.VMEM(spectra.shape, jnp.bfloat16),
+            pltpu.VMEM(ctf.shape, jnp.bfloat16),
+            pltpu.VMEM((2 * NF, 256), jnp.bfloat16),
+            pltpu.VMEM((rows_u, 128), jnp.float32),
+            pltpu.VMEM((n_grp, n_slab, slots), jnp.float32),
+            pltpu.VMEM((n_grp, n_slab, slots), jnp.float32),
+            pltpu.VMEM((256, ky_loc // 2 * NF), jnp.bfloat16),
+            pltpu.VMEM((n_grp, n_slab, cap, 128), jnp.bfloat16),
+            pltpu.VMEM((n_grp, n_slab * cap, 128), jnp.bfloat16),
+            pltpu.VMEM(spectra.shape, jnp.bfloat16),
+            pltpu.VMEM((PART_DEV * rows_u, 2 * NF), jnp.bfloat16),
+            pltpu.VMEM((n_grp, PART_DEV, 128), jnp.float32),
+            pltpu.VMEM((n_grp, PART_DEV, 128), jnp.float32),
+            dma((5,)),
+            dma((chunks,)),
+            dma((n_slab, n_grp)),
+            dma((n_slab, n_grp)),
+            dma((n_grp, n_slab)),
+            dma((n_grp, n_slab)),
+            dma((n_grp,)),
+            dma((n_grp,)),
+        ],
+        compiler_params=pltpu.CompilerParams(
+            collective_id=collective_id, has_side_effects=True, vmem_limit_bytes=48 * 2**20),
+    )(
+        class_ids, ori_count, send_map[0, 0], index[:, 0], frac[0], pencils, jnp.asarray(dft_table()),
+        spectra, ctf, jnp.asarray(column_phases()), jnp.asarray(row_phases()),
+    )
+
+
+def listed(n_slab, n_grp, *args):
+    scores, load = run_fused(n_slab, n_grp, CAP_FAST, 1, args)
+    return lax.cond(
+        load[0, 0] > CAP_FAST,
+        lambda: run_fused(n_slab, n_grp, n_slab * CAP, 2, args)[0],
+        lambda: scores,
+    )
+
+
 def solution(mesh):
+    n_slab, n_grp = mesh.shape["slab"], mesh.shape["grp"]
+
+    def body(*args):
+        if n_slab * CAP == 128 and n_grp == 4:
+            return listed(n_slab, n_grp, *args)
+        return shards(*args)
+
     return jax.shard_map(
-        shards,
+        body,
         mesh=mesh,
         in_specs=(
             P("slab", "grp", None),

time: 356 us -> 32.8 us (0.09)
  local copies, waits for them, and re-layouts: 107 us -> 1.15 us
  waiting for transfers between devices: 81.2 us -> 0 us
  blocking collectives: 53.7 us -> 0 us
  matrix products: 40.7 us -> 0 us
  Pallas kernels: 0 us -> 29.6 us
  loops' own time: 27.2 us -> 0.23 us
  other arithmetic: 24.7 us -> 0 us
  between operations: 13.7 us -> 1.61 us
  starting transfers between devices: 5.27 us -> 0 us
    all_gather x1 -> x0, waiting for transfers between devices: 57.9 us -> none  [shards(): gathered = lax.all_gather(slab_planes, 'grp', axis=3, tiled=True)]
    all_to_all x1 -> x0, blocking collectives: 53.7 us -> none  [shards(): lax.all_to_all(planes, 'slab', split_axis=0, concat_axis=1, tiled=True)]
    dot_general x13 -> x0, matrix products: 40.7 us -> none  [the longest x8 27 us: shift_score(): lax.dot_general(weighted, flat_refs, (((1,), (1,)), ((), ())), preferred_...]
    while x8 -> x0, local copies, waits for them, and re-layouts: 35.9 us -> none
    pallas_call x0 -> x1, Pallas kernels: none -> 29.6 us  [run_fused(): pl.pallas_call(lambda *refs: fused(n_slab, n_grp, cap, *refs), out_shape=...]
    another operation x1, loops' own time: 27.2 us -> 0.23 us  [listed(): lax.cond(load[0, 0] > CAP_FAST, lambda: run_fused(n_slab, n_grp, n_slab *...]
    unnamed x17 -> x21, local copies, waits for them, and re-layouts: 21.8 us -> 0.64 us
    another operation x9 -> x0, other arithmetic: 17.9 us -> none
  transfers between devices with their start and end apart: 3 -> 0, of which waited for: 3 -> 0; matrix products, arithmetic and copies ran while one was open for 0% -> 0% of each run, Pallas kernels for 0% -> 0%
where the time goes in v1:
time: 32.8 us; the launch traced here: 32.6 us
  Pallas kernels  29.6 us (90%)
  between operations  1.61 us (5%)
  local copies, waits for them, and re-layouts  1.15 us (4%)
    pallas_call x1, Pallas kernels, run_fused(): pl.pallas_call(lambda *refs: fused(n_slab, n_grp, cap, *refs), out_shape=...  29.6 us

profile of v1, /device:TPU:1, one launch (start us, length us, event | category | flops | bytes accessed | tf_op | source)
XLA Modules:
  0.0 32.6 jit_solution(16416026667962336078)
XLA Ops:
  0.0 0.0 copy-start.5
  0.0 0.0 copy-start.4
  0.0 0.0 copy-start.3
  0.0 0.0 copy-start.2
  0.0 0.0 copy-start.9
  0.0 0.0 copy-start.1
  0.0 0.0 copy-start.8
  0.0 0.0 copy-start.6
  0.1 0.0 copy-start.7
  0.1 0.0 copy-start
  0.9 29.6 %shard_map.138 = (f32[8,128]{1,0:T(8,128)S(1)}, f32[8,128]{1,0:T(8,128)S(1)}) custom-call(s32[8]{0:T(128)} %refs_0_.1, s32[1]{0:T(128)S(6)} %copy.21.refs_1_, s32[8,16]{1,0:T(8,128)} %bitcast.10, s32[2,8,64]{2,1,0:T(8,128)} %bitcast.8, f32[8,64]{1,0:T(8,128)} %bitcast.12, f32[32,64,512]{2,1,0:T(8,128)} %refs_5_.1, bf16[512,512]{1,0:T(8,128)(2,1)} %constant.9.clone.refs_6_, ...), custom_call_target="tpu_custom_call" | custom-call | tf_op jit(solution)/shard_map/pallas_call | solution.py:382
  30.5 0.5 %slice.3 = f32[1,1]{1,0:T(1,128)} slice(f32[8,128]{1,0:T(8,128)S(1)} %get-tuple-element.45), slice={[0:1], [0:1]} | slice | bytes 8 | tf_op jit(solution)/shard_map/slice | solution.py:428
  31.6 0.0 copy-done.5
  31.7 0.0 copy-done.4
  31.7 0.0 copy-done.3
  31.7 0.0 copy-done.2
  31.7 0.0 copy-done.9
  31.7 0.0 copy-done.1
  31.7 0.0 copy-done.8
  31.7 0.0 copy-done.6
  31.7 0.0 copy-done.7
  31.7 0.0 copy-done
  31.7 0.2 conditional.1
  32.0 0.6 %copy.22 = f32[8,128]{1,0:T(8,128)} copy(f32[8,128]{1,0:T(8,128)S(1)} %get-tuple-element.47) | data formatting | bytes 8192
Async XLA Ops:
  0.0 31.6 %copy-start.5 = (f32[256,128]{1,0:T(8,128)S(1)}, f32[256,128]{1,0:T(8,128)}, u32[]{:S(2)}) copy-start(f32[256,128]{1,0:T(8,128)} %constant.11.clone.refs_10_) | copy-start | bytes 393220
  0.0 31.7 %copy-start.4 = (bf16[512,256]{1,0:T(8,128)(2,1)S(1)}, bf16[512,256]{1,0:T(8,128)(2,1)}, u32[]{:S(2)}) copy-start(bf16[512,256]{1,0:T(8,128)(2,1)} %constant.10.clone.refs_9_) | copy-start | bytes 786436
  0.0 31.7 %copy-start.3 = (bf16[512,512]{1,0:T(8,128)(2,1)S(1)}, bf16[512,512]{1,0:T(8,128)(2,1)}, u32[]{:S(2)}) copy-start(bf16[512,512]{1,0:T(8,128)(2,1)} %constant.9.clone.refs_6_) | copy-start | bytes 1572868
  0.0 31.7 %copy-start.2 = (bf16[16,64,256]{2,1,0:T(8,128)(2,1)S(1)}, bf16[16,64,256]{2,1,0:T(8,128)(2,1)}, u32[]{:S(2)}) copy-start(bf16[16,64,256]{2,1,0:T(8,128)(2,1)} %refs_8_.1) | copy-start | bytes 1572868
  0.0 31.7 %copy-start.9 = (s32[8]{0:T(128)S(1)}, s32[8]{0:T(128)}, u32[]{:S(2)}) copy-start(s32[8]{0:T(128)} %refs_0_.1) | copy-start | bytes 100
  0.0 31.7 %copy-start.1 = (bf16[8,64,512]{2,1,0:T(8,128)(2,1)S(1)}, bf16[8,64,512]{2,1,0:T(8,128)(2,1)}, u32[]{:S(2)}) copy-start(bf16[8,64,512]{2,1,0:T(8,128)(2,1)} %refs_7_.1) | copy-start | bytes 1572868
  0.0 31.7 %copy-start.8 = (f32[1,8,64]{2,1,0:T(8,128)S(1)}, f32[1,8,64]{2,1,0:T(8,128)}, u32[]{:S(2)}) copy-start(f32[1,8,64]{2,1,0:T(8,128)} %param.19) | copy-start | bytes 6148
  0.0 31.7 %copy-start.6 = (s32[2,1,8,64]{3,2,1,0:T(8,128)S(1)}, s32[2,1,8,64]{3,2,1,0:T(8,128)}, u32[]{:S(2)}) copy-start(s32[2,1,8,64]{3,2,1,0:T(8,128)} %param.18) | copy-start | bytes 12292
  0.1 31.7 %copy-start.7 = (s32[1,1,8,16]{3,2,1,0:T(8,128)S(1)}, s32[1,1,8,16]{3,2,1,0:T(8,128)}, u32[]{:S(2)}) copy-start(s32[1,1,8,16]{3,2,1,0:T(8,128)} %param.17) | copy-start | bytes 1540
  0.1 31.7 %copy-start = (f32[32,64,512]{2,1,0:T(8,128)S(1)}, f32[32,64,512]{2,1,0:T(8,128)}, u32[]{:S(2)}) copy-start(f32[32,64,512]{2,1,0:T(8,128)} %refs_5_.1) | copy-start | bytes 12582916

commit v2 on v1

--- a/solution.py
+++ b/solution.py
@@ -177,32 +177,20 @@
              (phase_u.at[pl.ds(pl.multiple_of(g * rows_u, rows_u), rows_u)], row_ph)]
         )
     ]
-    line_loads = [
-        pltpu.make_async_copy(pencils.at[pl.ds(c * step, step)], lines.at[c], line_sem.at[c])
-        for c in range(chunks)
-    ]
+
+    def line_load(c):
+        return pltpu.make_async_copy(pencils.at[pl.ds(c * step, step)], lines.at[c], line_sem.at[c])
+
     loads[0].start()
-    for copy in line_loads:
-        copy.start()
+    for c in range(chunks):
+        line_load(c).start()
     for copy in loads[1:]:
         copy.start()
     own_map = send_map[...]
     maps[s, g] = jnp.concatenate([own_map] * n_slab, axis=1)
 
-    pl.semaphore_wait(barrier, len(peers))
-
-    def map_copy(to, whose):
-        return pltpu.make_async_remote_copy(
-            src_ref=maps.at[s, g], dst_ref=maps.at[whose[0], whose[1]],
-            send_sem=map_send.at[to[0], to[1]], recv_sem=map_recv.at[whose[0], whose[1]],
-            device_id=to, device_id_type=MESH)
-
-    for dg, ds in peers:
-        map_copy(peer(dg, ds), (s, g)).start()
-
-    loads[0].wait()
-    for c in range(chunks):
-        line_loads[c].wait()
+    def transform(c, carry):
+        line_load(c).wait()
         block = lines[c].reshape(step * kx_loc, 2 * NF).astype(jnp.bfloat16)
         lanes = lax.dot_general(
             table_w[...], block, (((1,), (1,)), ((), ())), preferred_element_type=jnp.float32
@@ -210,6 +198,22 @@
         for h in range(step // 2):
             planes[c * (step // 2) + h, :, :128] = lanes[:NF, h * 128:(h + 1) * 128]
             planes[c * (step // 2) + h, :, 128:] = lanes[NF:, h * 128:(h + 1) * 128]
+        return carry
+
+    loads[0].wait()
+    lax.fori_loop(0, chunks // 2, transform, 0)
+    pl.semaphore_wait(barrier, len(peers))
+
+    def map_copy(to, whose):
+        return pltpu.make_async_remote_copy(
+            src_ref=maps.at[s, g], dst_ref=maps.at[whose[0], whose[1]],
+            send_sem=map_send.at[to[0], to[1]], recv_sem=map_recv.at[whose[0], whose[1]],
+            device_id=to, device_id_type=MESH)
+
+    for dg, ds in peers:
+        map_copy(peer(dg, ds), (s, g)).start()
+
+    lax.fori_loop(chunks // 2, chunks, transform, 0)
 
     for dg, ds in peers:
         whose = peer(dg, ds)
@@ -242,7 +246,7 @@
     most = jnp.zeros((rows.shape[0], 1), jnp.float32)
     for a in range(n_slab):
         most = jnp.maximum(most, jnp.sum(jnp.where(home == a, 1.0, 0.0), axis=1, keepdims=True))
-    load_out[...] = jnp.broadcast_to(jnp.max(most, axis=0, keepdims=True), load_out.shape)
+    load_out[0] = (jnp.max(most) > cap).astype(jnp.int32)
 
     def row_copy(to, whose):
         return pltpu.make_async_remote_copy(
@@ -255,8 +259,9 @@
     at_once = 256 // cap
     lane256 = iota((256, NF), 1)
     lane128 = iota((256, 128), 1)
-    for dg in [1, 2, 3, 0][:n_grp]:
-        to_g = lax.rem(g + dg, n_grp)
+
+    def pick(i, carry):
+        to_g = lax.rem(g + i + 1, n_grp)
         for q in range(n_slab // at_once):
             rk = rank_ref[to_g, q * at_once:(q + 1) * at_once]
             cd = key_ref[to_g, q * at_once:(q + 1) * at_once]
@@ -264,10 +269,11 @@
             hit = jnp.where(rk[:, None, :] == places, cd[:, None, :], 0.0)
             found = (jnp.sum(hit, axis=2, keepdims=True) - 1.0).reshape(256, 1).astype(jnp.int32)
             odd = (found & 1) == 1
-            where_row = found >> 1
+            pair = jnp.broadcast_to((found >> (NF.bit_length())).astype(jnp.float32), (256, NF)).astype(jnp.bfloat16)
+            plane_hit = jnp.where(((found >> 1) & (NF - 1)) == lane256, 1.0, 0.0).astype(jnp.bfloat16)
             for j in range(pairs):
                 picked[:, j * NF:(j + 1) * NF] = jnp.where(
-                    where_row - j * NF == lane256, 1.0, 0.0).astype(jnp.bfloat16)
+                    pair == jnp.bfloat16(j), plane_hit, jnp.bfloat16(0))
             got = jnp.dot(picked[...], planes[...].reshape(pairs * NF, 256),
                           preferred_element_type=jnp.float32)
             a, b = got[:, :128], got[:, 128:]
@@ -275,8 +281,16 @@
                             jnp.where(odd, b, pltpu.roll(b, 64, 1)))
             sendbuf[to_g, q * at_once:(q + 1) * at_once] = row.astype(jnp.bfloat16).reshape(at_once, cap, 128)
         for ds in range(n_slab):
-            if dg + ds > 0:
-                row_copy(peer(dg, ds), (s, g)).start()
+            to = (lax.rem(s + ds, n_slab), to_g)
+            if ds > 0:
+                row_copy(to, (s, g)).start()
+            else:
+                @pl.when(i < n_grp - 1)
+                def _():
+                    row_copy(to, (s, g)).start()
+        return carry
+
+    lax.fori_loop(0, n_grp, pick, 0)
     recv[g, pl.ds(pl.multiple_of(s * cap, cap), cap)] = sendbuf[g, s]
 
     for copy in loads[1:]:
@@ -297,6 +311,8 @@
     place = jnp.sum(ones * (own_rank + base + 1.0), axis=0, keepdims=True) - 1.0
     spread = jnp.where(place == iota((n_slab * cap, slots), 0).astype(jnp.float32), 1.0, 0.0).astype(jnp.bfloat16)
 
+    for dg, ds in peers:
+        map_copy(peer(dg, ds), (s, g)).wait_send()
     for dg, ds in peers:
         whose = peer(dg, ds)
         row_copy(whose, whose).wait_recv()
@@ -322,8 +338,9 @@
     slot_id = iota((slots, rows_u), 0)
     live = ori_count[0]
     lane_p = iota((PART_DEV, 128), 1)
-    for dg in [1, 2, 3, 0][:n_grp]:
-        to_g = lax.rem(g + dg, n_grp)
+
+    def score(i, carry):
+        to_g = lax.rem(g + i + 1, n_grp)
         folded = []
         for half in range(2):
             o = to_g * 2 + half
@@ -348,21 +365,23 @@
             t = (t + pltpu.roll(t, 64, 1)) * (1.0 / NF)
             folded.append(jnp.where(o < live, t, 0.0))
         block = jnp.where(lane_p < 64, folded[0], folded[1])
-        if dg > 0:
-            part_send[to_g] = block
+        part_send[to_g] = block
+
+        @pl.when(i < n_grp - 1)
+        def _():
             sum_copy(to_g, g).start()
-        else:
-            total = block
+
+        return carry
+
+    lax.fori_loop(0, n_grp, score, 0)
+    for dg, ds in peers:
+        row_copy(peer(dg, ds), (s, g)).wait_send()
+    total = part_send[g]
     for dg in range(1, n_grp):
         from_g = lax.rem(g + dg, n_grp)
         sum_copy(from_g, from_g).wait_recv()
         total += part_recv[from_g]
     out[...] = total
-
-    for dg, ds in peers:
-        to = peer(dg, ds)
-        map_copy(to, (s, g)).wait_send()
-        row_copy(to, (s, g)).wait_send()
     for dg in range(1, n_grp):
         sum_copy(lax.rem(g + dg, n_grp), g).wait_send()
 
@@ -383,10 +402,10 @@
         lambda *refs: fused(n_slab, n_grp, cap, *refs),
         out_shape=[
             jax.ShapeDtypeStruct((PART_DEV, ORI_MAX * TRANS // n_grp), jnp.float32),
-            jax.ShapeDtypeStruct((8, 128), jnp.float32),
+            jax.ShapeDtypeStruct((1,), jnp.int32),
         ],
         in_specs=[smem, smem, vmem, vmem, vmem, hbm, hbm, hbm, hbm, hbm, hbm],
-        out_specs=[vmem, vmem],
+        out_specs=[vmem, smem],
         scratch_shapes=[
             pltpu.VMEM((n_slab, n_grp, n_slab, slots), jnp.int32),
             pltpu.VMEM((chunks, 4, kx_loc, 2 * NF), jnp.float32),
@@ -415,7 +434,7 @@
             dma((n_grp,)),
         ],
         compiler_params=pltpu.CompilerParams(
-            collective_id=collective_id, has_side_effects=True, vmem_limit_bytes=48 * 2**20),
+            collective_id=collective_id, has_side_effects=True, vmem_limit_bytes=60 * 2**20),
     )(
         class_ids, ori_count, send_map[0, 0], index[:, 0], frac[0], pencils, jnp.asarray(dft_table()),
         spectra, ctf, jnp.asarray(column_phases()), jnp.asarray(row_phases()),
@@ -425,7 +444,7 @@
 def listed(n_slab, n_grp, *args):
     scores, load = run_fused(n_slab, n_grp, CAP_FAST, 1, args)
     return lax.cond(
-        load[0, 0] > CAP_FAST,
+        load.reshape(()) > 0,
         lambda: run_fused(n_slab, n_grp, n_slab * CAP, 2, args)[0],
         lambda: scores,
     )

time: 32.8 us -> 31.4 us (0.957)
  local copies, waits for them, and re-layouts: 1.15 us -> 0.63 us
  Pallas kernels: 29.6 us -> 29.1 us
    pallas_call x1, Pallas kernels: 29.6 us -> 29.1 us  [run_fused(): pl.pallas_call(lambda *refs: fused(n_slab, n_grp, cap, *refs), out_shape=...]
    slice x1 -> x0, local copies, waits for them, and re-layouts: 0.51 us -> none  [listed(): load[0, 0] > CAP_FAST]
where the time goes in v2:
time: 31.4 us; the launch traced here: 31.2 us
  Pallas kernels  29.1 us (93%)
  between operations  1.56 us (5%)
  local copies, waits for them, and re-layouts  0.63 us (2%)
    pallas_call x1, Pallas kernels, run_fused(): pl.pallas_call(lambda *refs: fused(n_slab, n_grp, cap, *refs), out_shape=...  29.1 us
    unnamed x19, local copies, waits for them, and re-layouts  0.63 us

profile of v2, /device:TPU:1, one launch (start us, length us, event | category | flops | bytes accessed | tf_op | source)
XLA Modules:
  0.0 31.2 jit_solution(16439054971268226752)
XLA Ops:
  0.0 0.0 copy-start.4
  0.0 0.0 copy-start.3
  0.0 0.0 copy-start.2
  0.0 0.0 copy-start.1
  0.0 0.0 copy-start.8
  0.0 0.0 copy-start
  0.0 0.0 copy-start.7
  0.0 0.0 copy-start.5
  0.1 0.0 copy-start.6
  0.9 29.1 %shard_map.138 = (f32[8,128]{1,0:T(8,128)S(1)}, s32[1]{0:T(128)}) custom-call(s32[8]{0:T(128)} %refs_0_.1, s32[1]{0:T(128)S(6)} %copy.21.refs_1_, s32[8,16]{1,0:T(8,128)} %bitcast.10, s32[2,8,64]{2,1,0:T(8,128)} %bitcast.8, f32[8,64]{1,0:T(8,128)} %bitcast.12, f32[32,64,512]{2,1,0:T(8,128)} %refs_5_.1, bf16[512,512]{1,0:T(8,128)(2,1)} %constant.9.clone.refs_6_, ...), custom_call_target="tpu_custom_call" | custom-call | tf_op jit(solution)/shard_map/pallas_call | solution.py:401
  30.5 0.0 copy-done.4
  30.6 0.0 copy-done.3
  30.6 0.0 copy-done.2
  30.6 0.0 copy-done.1
  30.6 0.0 copy-done.8
  30.6 0.0 copy-done
  30.6 0.0 copy-done.7
  30.6 0.0 copy-done.5
  30.6 0.0 copy-done.6
  30.7 0.6 %copy.22 = f32[8,128]{1,0:T(8,128)} copy(f32[8,128]{1,0:T(8,128)S(1)} %get-tuple-element.47) | data formatting | bytes 8192
  (1 shorter events, 0.0 us)
Async XLA Ops:
  0.0 30.5 %copy-start.4 = (f32[256,128]{1,0:T(8,128)S(1)}, f32[256,128]{1,0:T(8,128)}, u32[]{:S(2)}) copy-start(f32[256,128]{1,0:T(8,128)} %constant.11.clone.refs_10_) | copy-start | bytes 393220
  0.0 30.6 %copy-start.3 = (bf16[512,256]{1,0:T(8,128)(2,1)S(1)}, bf16[512,256]{1,0:T(8,128)(2,1)}, u32[]{:S(2)}) copy-start(bf16[512,256]{1,0:T(8,128)(2,1)} %constant.10.clone.refs_9_) | copy-start | bytes 786436
  0.0 30.6 %copy-start.2 = (bf16[512,512]{1,0:T(8,128)(2,1)S(1)}, bf16[512,512]{1,0:T(8,128)(2,1)}, u32[]{:S(2)}) copy-start(bf16[512,512]{1,0:T(8,128)(2,1)} %constant.9.clone.refs_6_) | copy-start | bytes 1572868
  0.0 30.6 %copy-start.1 = (bf16[16,64,256]{2,1,0:T(8,128)(2,1)S(1)}, bf16[16,64,256]{2,1,0:T(8,128)(2,1)}, u32[]{:S(2)}) copy-start(bf16[16,64,256]{2,1,0:T(8,128)(2,1)} %refs_8_.1) | copy-start | bytes 1572868
  0.0 30.6 %copy-start.8 = (s32[8]{0:T(128)S(1)}, s32[8]{0:T(128)}, u32[]{:S(2)}) copy-start(s32[8]{0:T(128)} %refs_0_.1) | copy-start | bytes 100
  0.0 30.6 %copy-start = (bf16[8,64,512]{2,1,0:T(8,128)(2,1)S(1)}, bf16[8,64,512]{2,1,0:T(8,128)(2,1)}, u32[]{:S(2)}) copy-start(bf16[8,64,512]{2,1,0:T(8,128)(2,1)} %refs_7_.1) | copy-start | bytes 1572868
  0.0 30.6 %copy-start.7 = (f32[1,8,64]{2,1,0:T(8,128)S(1)}, f32[1,8,64]{2,1,0:T(8,128)}, u32[]{:S(2)}) copy-start(f32[1,8,64]{2,1,0:T(8,128)} %param.19) | copy-start | bytes 6148
  0.0 30.6 %copy-start.5 = (s32[2,1,8,64]{3,2,1,0:T(8,128)S(1)}, s32[2,1,8,64]{3,2,1,0:T(8,128)}, u32[]{:S(2)}) copy-start(s32[2,1,8,64]{3,2,1,0:T(8,128)} %param.18) | copy-start | bytes 12292
  0.1 30.6 %copy-start.6 = (s32[1,1,8,16]{3,2,1,0:T(8,128)S(1)}, s32[1,1,8,16]{3,2,1,0:T(8,128)}, u32[]{:S(2)}) copy-start(s32[1,1,8,16]{3,2,1,0:T(8,128)} %param.17) | copy-start | bytes 1540

commit v3 on v2

--- a/solution.py
+++ b/solution.py
@@ -134,7 +134,8 @@
     full = np.block([[cos, -sin], [sin, cos]]).astype(np.float32)
     high = full.astype(jnp.bfloat16)
     low = (full - high.astype(np.float32)).astype(jnp.bfloat16)
-    return np.concatenate([high, low], axis=1)
+    both = np.concatenate([high, low], axis=1).reshape(2, 2, 128, 256)
+    return both.transpose(1, 0, 2, 3).reshape(2, NF, 256)
 
 
 def row_phases():
@@ -150,10 +151,10 @@
 
 def fused(
     n_slab, n_grp, cap,
-    class_ids, ori_count, send_map, index, frac, pencils, dft, spectra, ctf, phase_v, phase_u,
+    class_hbm, count_hbm, map_hbm, index_hbm, frac_hbm, pencils, dft, spectra, ctf, phase_v, phase_u,
     out, load_out,
-    maps, lines, table_w, planes, spec_in, ctf_in, col_ph, row_ph, rank_ref, key_ref, picked, sendbuf,
-    recv, weighted, product, part_send, part_recv,
+    maps, lines, table_w, planes, spec_in, ctf_in, col_ph, row_ph, rank_ref, key_ref, picked2, sendbuf,
+    recv, weighted, product, part_send, part_recv, class_ids, ori_count, send_map, index, frac,
     load_sem, line_sem, map_send, map_recv, row_send, row_recv, sum_send, sum_recv,
 ):
     s, g = lax.axis_index("slab"), lax.axis_index("grp")
@@ -164,6 +165,9 @@
     step = ky_loc // chunks
     peers = [(dg, ds) for dg in range(n_grp) for ds in range(n_slab) if dg + ds > 0]
 
+    x, core = g // 2, g % 2
+    order = [(1 - x) * 2 + core, (1 - x) * 2 + 1 - core, x * 2 + 1 - core, g]
+
     def peer(dg, ds):
         return lax.rem(s + ds, n_slab), lax.rem(g + dg, n_grp)
 
@@ -173,7 +177,8 @@
     loads = [
         pltpu.make_async_copy(a, b, load_sem.at[i])
         for i, (a, b) in enumerate(
-            [(dft, table_w), (ctf, ctf_in), (spectra, spec_in), (phase_v, col_ph),
+            [(map_hbm, send_map), (dft, table_w), (class_hbm, class_ids), (count_hbm, ori_count),
+             (index_hbm, index), (frac_hbm, frac), (ctf, ctf_in), (spectra, spec_in), (phase_v, col_ph),
              (phase_u.at[pl.ds(pl.multiple_of(g * rows_u, rows_u), rows_u)], row_ph)]
         )
     ]
@@ -181,13 +186,12 @@
     def line_load(c):
         return pltpu.make_async_copy(pencils.at[pl.ds(c * step, step)], lines.at[c], line_sem.at[c])
 
-    loads[0].start()
+    for copy in loads[:2]:
+        copy.start()
     for c in range(chunks):
         line_load(c).start()
-    for copy in loads[1:]:
+    for copy in loads[2:]:
         copy.start()
-    own_map = send_map[...]
-    maps[s, g] = jnp.concatenate([own_map] * n_slab, axis=1)
 
     def transform(c, carry):
         line_load(c).wait()
@@ -200,8 +204,11 @@
             planes[c * (step // 2) + h, :, 128:] = lanes[NF:, h * 128:(h + 1) * 128]
         return carry
 
+    loads[1].wait()
+    for c in range(chunks // 2):
+        transform(c, 0)
     loads[0].wait()
-    lax.fori_loop(0, chunks // 2, transform, 0)
+    maps[s, g] = jnp.concatenate([send_map[...]] * n_slab, axis=1)
     pl.semaphore_wait(barrier, len(peers))
 
     def map_copy(to, whose):
@@ -213,7 +220,8 @@
     for dg, ds in peers:
         map_copy(peer(dg, ds), (s, g)).start()
 
-    lax.fori_loop(chunks // 2, chunks, transform, 0)
+    for c in range(chunks // 2, chunks):
+        transform(c, 0)
 
     for dg, ds in peers:
         whose = peer(dg, ds)
@@ -260,8 +268,9 @@
     lane256 = iota((256, NF), 1)
     lane128 = iota((256, 128), 1)
 
-    def pick(i, carry):
-        to_g = lax.rem(g + i + 1, n_grp)
+    def pick(i):
+        to_g = order[i]
+        picked = picked2.at[i % 2]
         for q in range(n_slab // at_once):
             rk = rank_ref[to_g, q * at_once:(q + 1) * at_once]
             cd = key_ref[to_g, q * at_once:(q + 1) * at_once]
@@ -280,27 +289,24 @@
             row = jnp.where(lane128 < 64, jnp.where(odd, pltpu.roll(a, 64, 1), a),
                             jnp.where(odd, b, pltpu.roll(b, 64, 1)))
             sendbuf[to_g, q * at_once:(q + 1) * at_once] = row.astype(jnp.bfloat16).reshape(at_once, cap, 128)
-        for ds in range(n_slab):
-            to = (lax.rem(s + ds, n_slab), to_g)
-            if ds > 0:
-                row_copy(to, (s, g)).start()
-            else:
-                @pl.when(i < n_grp - 1)
-                def _():
-                    row_copy(to, (s, g)).start()
-        return carry
-
-    lax.fori_loop(0, n_grp, pick, 0)
+        for ds in sorted(range(n_slab), key=lambda d: -min(d, n_slab - d)):
+            if i < n_grp - 1 or ds > 0:
+                row_copy((lax.rem(s + ds, n_slab), to_g), (s, g)).start()
+
+    for i in range(n_grp):
+        pick(i)
     recv[g, pl.ds(pl.multiple_of(s * cap, cap), cap)] = sendbuf[g, s]
 
-    for copy in loads[1:]:
+    for copy in loads[2:]:
         copy.wait()
     for p in range(PART_DEV):
-        ctf_rows = ctf_in[class_ids[p]].astype(jnp.float32)
-        for part in range(2):
-            weighted[p, :, part * NF:(part + 1) * NF] = (
-                ctf_rows * spec_in[p, :, part * NF:(part + 1) * NF].astype(jnp.float32)
-            ).astype(jnp.bfloat16)
+        for h in range(2):
+            ctf_rows = ctf_in[class_ids[p], :, h * 128:(h + 1) * 128].astype(jnp.float32)
+            for part in range(2):
+                at = part * NF + h * 128
+                weighted[h, p, :, part * 128:(part + 1) * 128] = (
+                    ctf_rows * spec_in[p, :, at:at + 128].astype(jnp.float32)
+                ).astype(jnp.bfloat16)
 
     own = jnp.sum(jnp.where(lane // CAP == iota((n_slab, slots), 0), maps_row(maps, s, g, n_slab), 0),
                   axis=0, keepdims=True)
@@ -313,21 +319,19 @@
 
     for dg, ds in peers:
         map_copy(peer(dg, ds), (s, g)).wait_send()
-    for dg, ds in peers:
-        whose = peer(dg, ds)
-        row_copy(whose, whose).wait_recv()
-    lists = [
-        lax.dot_general(spread, recv[b], (((0,), (0,)), ((), ())), preferred_element_type=jnp.float32)
-        for b in range(n_grp)
-    ]
     lane_s = iota((slots, 128), 1)
-    real, imag = [], []
-    for b in range(0, n_grp, 2):
-        x, y = lists[b], lists[b + 1]
-        real.append(jnp.where(lane_s < 64, x, pltpu.roll(y, 64, 1)))
-        imag.append(jnp.where(lane_s < 64, pltpu.roll(x, 64, 1), y))
-    received = jnp.concatenate(real + imag, axis=1).astype(jnp.bfloat16)
-    received = jnp.concatenate([received, received], axis=0)
+
+    def lists(half, turn):
+        got = []
+        for b in range(2):
+            from_g = half * 2 + b
+            got.append(lax.dot_general(spread, recv[from_g], (((0,), (0,)), ((), ())),
+                                       preferred_element_type=jnp.float32))
+        a, b = got
+        block = jnp.concatenate([jnp.where(lane_s < 64, a, pltpu.roll(b, 64, 1)),
+                                 jnp.where(lane_s < 64, pltpu.roll(a, 64, 1), b)], axis=1)
+        block = block.astype(jnp.bfloat16)
+        return jnp.concatenate([block, block], axis=0)
 
     def sum_copy(to_g, whose_g):
         return pltpu.make_async_remote_copy(
@@ -339,41 +343,50 @@
     live = ori_count[0]
     lane_p = iota((PART_DEV, 128), 1)
 
-    def score(i, carry):
-        to_g = lax.rem(g + i + 1, n_grp)
-        folded = []
-        for half in range(2):
-            o = to_g * 2 + half
-            i0 = index[0, pl.ds(o, 1), :]
-            i1 = index[1, pl.ds(o, 1), :]
-            w = frac[pl.ds(o, 1), :]
-            taps = jnp.where(slot_id == i0, 1.0 - w, 0.0) + jnp.where(slot_id == i1, w, 0.0)
-            high = taps.astype(jnp.bfloat16)
-            low = (taps - high.astype(jnp.float32)).astype(jnp.bfloat16)
-            rows_o = lax.dot_general(
-                jnp.concatenate([high, low], axis=0), received, (((0,), (0,)), ((), ())),
-                preferred_element_type=jnp.float32)
-            sr, si = rows_o[:, :NF], rows_o[:, NF:]
-            for p in range(PART_DEV):
-                wr = weighted[p, :, :NF].astype(jnp.float32)
-                wi = weighted[p, :, NF:].astype(jnp.float32)
-                product[p * rows_u:(p + 1) * rows_u, :NF] = (wr * sr + wi * si).astype(jnp.bfloat16)
-                product[p * rows_u:(p + 1) * rows_u, NF:] = (wr * si - wi * sr).astype(jnp.bfloat16)
-            z = jnp.dot(product[...], col_ph[...], preferred_element_type=jnp.float32)
-            z = (z[:, :128] + z[:, 128:]).reshape(PART_DEV, rows_u, 128)
-            t = jnp.sum(z * row_ph[...][None], axis=1)
-            t = (t + pltpu.roll(t, 64, 1)) * (1.0 / NF)
-            folded.append(jnp.where(o < live, t, 0.0))
-        block = jnp.where(lane_p < 64, folded[0], folded[1])
-        part_send[to_g] = block
-
-        @pl.when(i < n_grp - 1)
-        def _():
-            sum_copy(to_g, g).start()
-
-        return carry
-
-    lax.fori_loop(0, n_grp, score, 0)
+    def half_score(o, half, received, buf):
+        i0 = index[0, pl.ds(o, 1), :]
+        i1 = index[1, pl.ds(o, 1), :]
+        w = frac[pl.ds(o, 1), :]
+        taps = jnp.where(slot_id == i0, 1.0 - w, 0.0) + jnp.where(slot_id == i1, w, 0.0)
+        high = taps.astype(jnp.bfloat16)
+        low = (taps - high.astype(jnp.float32)).astype(jnp.bfloat16)
+        rows_o = lax.dot_general(
+            jnp.concatenate([high, low], axis=0), received, (((0,), (0,)), ((), ())),
+            preferred_element_type=jnp.float32)
+        sr, si = rows_o[:, :128], rows_o[:, 128:]
+        for p in range(PART_DEV):
+            wr = weighted[half, p, :, :128].astype(jnp.float32)
+            wi = weighted[half, p, :, 128:].astype(jnp.float32)
+            product[buf, p * rows_u:(p + 1) * rows_u, :128] = (wr * sr + wi * si).astype(jnp.bfloat16)
+            product[buf, p * rows_u:(p + 1) * rows_u, 128:] = (wr * si - wi * sr).astype(jnp.bfloat16)
+        z = jnp.dot(product[buf], col_ph[half], preferred_element_type=jnp.float32)
+        z = (z[:, :128] + z[:, 128:]).reshape(PART_DEV, rows_u, 128)
+        return jnp.sum(z * row_ph[...][None], axis=1)
+
+    partial = {}
+    for turn, half in enumerate([1 - x, x]):
+        for i in (0, 1) if turn == 0 else (2, 3):
+            for ds in range(n_slab):
+                if i < n_grp - 1 or ds > 0:
+                    whose = (lax.rem(s + ds, n_slab), order[i])
+                    row_copy(whose, whose).wait_recv()
+        received = lists(half, turn)
+        for i in range(n_grp):
+            to_g = order[i]
+            folded = []
+            for e in range(2):
+                o = to_g * 2 + e
+                t = half_score(o, half, received, e)
+                if turn == 0:
+                    partial[i, e] = t
+                else:
+                    t = partial[i, e] + t
+                    t = (t + pltpu.roll(t, 64, 1)) * (1.0 / NF)
+                    folded.append(jnp.where(o < live, t, 0.0))
+            if turn == 1:
+                part_send[to_g] = jnp.where(lane_p < 64, folded[0], folded[1])
+                if i < n_grp - 1:
+                    sum_copy(to_g, g).start()
     for dg, ds in peers:
         row_copy(peer(dg, ds), (s, g)).wait_send()
     total = part_send[g]
@@ -404,7 +417,7 @@
             jax.ShapeDtypeStruct((PART_DEV, ORI_MAX * TRANS // n_grp), jnp.float32),
             jax.ShapeDtypeStruct((1,), jnp.int32),
         ],
-        in_specs=[smem, smem, vmem, vmem, vmem, hbm, hbm, hbm, hbm, hbm, hbm],
+        in_specs=[hbm] * 11,
         out_specs=[vmem, smem],
         scratch_shapes=[
             pltpu.VMEM((n_slab, n_grp, n_slab, slots), jnp.int32),
@@ -413,18 +426,23 @@
             pltpu.VMEM((ky_loc // 2, NF, 256), jnp.bfloat16),
             pltpu.VMEM(spectra.shape, jnp.bfloat16),
             pltpu.VMEM(ctf.shape, jnp.bfloat16),
-            pltpu.VMEM((2 * NF, 256), jnp.bfloat16),
+            pltpu.VMEM((2, NF, 256), jnp.bfloat16),
             pltpu.VMEM((rows_u, 128), jnp.float32),
             pltpu.VMEM((n_grp, n_slab, slots), jnp.float32),
             pltpu.VMEM((n_grp, n_slab, slots), jnp.float32),
-            pltpu.VMEM((256, ky_loc // 2 * NF), jnp.bfloat16),
+            pltpu.VMEM((2, 256, ky_loc // 2 * NF), jnp.bfloat16),
             pltpu.VMEM((n_grp, n_slab, cap, 128), jnp.bfloat16),
             pltpu.VMEM((n_grp, n_slab * cap, 128), jnp.bfloat16),
-            pltpu.VMEM(spectra.shape, jnp.bfloat16),
-            pltpu.VMEM((PART_DEV * rows_u, 2 * NF), jnp.bfloat16),
+            pltpu.VMEM((2, PART_DEV, rows_u, NF), jnp.bfloat16),
+            pltpu.VMEM((2, PART_DEV * rows_u, NF), jnp.bfloat16),
             pltpu.VMEM((n_grp, PART_DEV, 128), jnp.float32),
             pltpu.VMEM((n_grp, PART_DEV, 128), jnp.float32),
-            dma((5,)),
+            pltpu.SMEM(class_ids.shape, jnp.int32),
+            pltpu.SMEM(ori_count.shape, jnp.int32),
+            pltpu.VMEM(send_map.shape[2:], jnp.int32),
+            pltpu.VMEM((2, ORI_MAX, rows_u), jnp.int32),
+            pltpu.VMEM((ORI_MAX, rows_u), jnp.float32),
+            dma((10,)),
             dma((chunks,)),
             dma((n_slab, n_grp)),
             dma((n_slab, n_grp)),

time: 31.4 us -> 30.7 us (0.978)
  Pallas kernels: 29.1 us -> 28.1 us
    pallas_call x1, Pallas kernels: 29.1 us -> 28.1 us  [run_fused(): pl.pallas_call(lambda *refs: fused(n_slab, n_grp, cap, *refs), out_shape=...]
where the time goes in v3:
time: 30.7 us; the launch traced here: 30.5 us
  Pallas kernels  28.1 us (92%)
  between operations  1.56 us (5%)
  local copies, waits for them, and re-layouts  0.63 us (2%)
    pallas_call x1, Pallas kernels, run_fused(): pl.pallas_call(lambda *refs: fused(n_slab, n_grp, cap, *refs), out_shape=...  28.1 us
    unnamed x19, local copies, waits for them, and re-layouts  0.63 us

profile of v3, /device:TPU:1, one launch (start us, length us, event | category | flops | bytes accessed | tf_op | source)
XLA Modules:
  0.0 30.5 jit_solution(14244942454708676756)
XLA Ops:
  0.0 0.0 copy-start.4
  0.0 0.0 copy-start.3
  0.0 0.0 copy-start.2
  0.0 0.0 copy-start.1
  0.0 0.0 copy-start.8
  0.0 0.0 copy-start
  0.0 0.0 copy-start.7
  0.0 0.0 copy-start.5
  0.1 0.0 copy-start.6
  0.9 28.1 %shard_map.138 = (f32[8,128]{1,0:T(8,128)S(1)}, s32[1]{0:T(128)}) custom-call(s32[8]{0:T(128)} %refs_0_.1, s32[1]{0:T(128)S(6)} %copy.21.refs_1_, s32[8,16]{1,0:T(8,128)} %bitcast.10, s32[2,8,64]{2,1,0:T(8,128)} %bitcast.8, f32[8,64]{1,0:T(8,128)} %bitcast.12, f32[32,64,512]{2,1,0:T(8,128)} %refs_5_.1, bf16[512,512]{1,0:T(8,128)(2,1)} %constant.9.clone.refs_6_, ...), custom_call_target="tpu_custom_call" | custom-call | tf_op jit(solution)/shard_map/pallas_call | solution.py:414
  29.6 0.0 copy-done.4
  29.6 0.0 copy-done.3
  29.6 0.0 copy-done.2
  29.6 0.0 copy-done.1
  29.6 0.0 copy-done.8
  29.6 0.0 copy-done
  29.7 0.0 copy-done.7
  29.7 0.0 copy-done.5
  29.7 0.0 copy-done.6
  29.7 0.2 conditional.1
  29.9 0.6 %copy.22 = f32[8,128]{1,0:T(8,128)} copy(f32[8,128]{1,0:T(8,128)S(1)} %get-tuple-element.47) | data formatting | bytes 8192
Async XLA Ops:
  0.0 29.6 %copy-start.4 = (f32[256,128]{1,0:T(8,128)S(1)}, f32[256,128]{1,0:T(8,128)}, u32[]{:S(2)}) copy-start(f32[256,128]{1,0:T(8,128)} %constant.11.clone.refs_10_) | copy-start | bytes 393220
  0.0 29.6 %copy-start.3 = (bf16[2,256,256]{2,1,0:T(8,128)(2,1)S(1)}, bf16[2,256,256]{2,1,0:T(8,128)(2,1)}, u32[]{:S(2)}) copy-start(bf16[2,256,256]{2,1,0:T(8,128)(2,1)} %constant.10.clone.refs_9_) | copy-start | bytes 786436
  0.0 29.6 %copy-start.2 = (bf16[512,512]{1,0:T(8,128)(2,1)S(1)}, bf16[512,512]{1,0:T(8,128)(2,1)}, u32[]{:S(2)}) copy-start(bf16[512,512]{1,0:T(8,128)(2,1)} %constant.9.clone.refs_6_) | copy-start | bytes 1572868
  0.0 29.6 %copy-start.1 = (bf16[16,64,256]{2,1,0:T(8,128)(2,1)S(1)}, bf16[16,64,256]{2,1,0:T(8,128)(2,1)}, u32[]{:S(2)}) copy-start(bf16[16,64,256]{2,1,0:T(8,128)(2,1)} %refs_8_.1) | copy-start | bytes 1572868
  0.0 29.6 %copy-start.8 = (s32[8]{0:T(128)S(1)}, s32[8]{0:T(128)}, u32[]{:S(2)}) copy-start(s32[8]{0:T(128)} %refs_0_.1) | copy-start | bytes 100
  0.0 29.6 %copy-start = (bf16[8,64,512]{2,1,0:T(8,128)(2,1)S(1)}, bf16[8,64,512]{2,1,0:T(8,128)(2,1)}, u32[]{:S(2)}) copy-start(bf16[8,64,512]{2,1,0:T(8,128)(2,1)} %refs_7_.1) | copy-start | bytes 1572868
  0.0 29.6 %copy-start.7 = (f32[1,8,64]{2,1,0:T(8,128)S(1)}, f32[1,8,64]{2,1,0:T(8,128)}, u32[]{:S(2)}) copy-start(f32[1,8,64]{2,1,0:T(8,128)} %param.19) | copy-start | bytes 6148
  0.0 29.6 %copy-start.5 = (s32[2,1,8,64]{3,2,1,0:T(8,128)S(1)}, s32[2,1,8,64]{3,2,1,0:T(8,128)}, u32[]{:S(2)}) copy-start(s32[2,1,8,64]{3,2,1,0:T(8,128)} %param.18) | copy-start | bytes 12292
  0.1 29.6 %copy-start.6 = (s32[1,1,8,16]{3,2,1,0:T(8,128)S(1)}, s32[1,1,8,16]{3,2,1,0:T(8,128)}, u32[]{:S(2)}) copy-start(s32[1,1,8,16]{3,2,1,0:T(8,128)} %param.17) | copy-start | bytes 1540

commit v4 on v3

--- a/solution.py
+++ b/solution.py
@@ -155,7 +155,7 @@
     out, load_out,
     maps, lines, table_w, planes, spec_in, ctf_in, col_ph, row_ph, rank_ref, key_ref, picked2, sendbuf,
     recv, weighted, product, part_send, part_recv, class_ids, ori_count, send_map, index, frac,
-    load_sem, line_sem, map_send, map_recv, row_send, row_recv, sum_send, sum_recv,
+    load_sem, line_sem, hop_send, hop_recv, map_send, map_recv, row_send, row_recv, sum_send, sum_recv,
 ):
     s, g = lax.axis_index("slab"), lax.axis_index("grp")
     ky_loc, kx_loc = pencils.shape[0], pencils.shape[1]
@@ -172,8 +172,20 @@
         return lax.rem(s + ds, n_slab), lax.rem(g + dg, n_grp)
 
     barrier = pltpu.get_barrier_semaphore()
-    for dg, ds in peers:
-        pl.semaphore_signal(barrier, inc=1, device_id=peer(dg, ds), device_id_type=MESH)
+    deep = n_slab // 2
+    z, y = s // 2, s % 2
+    beside = [(z * 2 + 1 - y, g)] + [peer(dg, 0) for dg in range(1, n_grp)]
+    for to in beside:
+        pl.semaphore_signal(barrier, inc=1, device_id=to, device_id_type=MESH)
+
+    @pl.when(z > 0)
+    def _():
+        pl.semaphore_signal(barrier, inc=1, device_id=(s - 2, g), device_id_type=MESH)
+
+    @pl.when(z < deep - 1)
+    def _():
+        pl.semaphore_signal(barrier, inc=1, device_id=(s + 2, g), device_id_type=MESH)
+
     loads = [
         pltpu.make_async_copy(a, b, load_sem.at[i])
         for i, (a, b) in enumerate(
@@ -204,34 +216,80 @@
             planes[c * (step // 2) + h, :, 128:] = lanes[NF:, h * 128:(h + 1) * 128]
         return carry
 
-    loads[1].wait()
-    for c in range(chunks // 2):
-        transform(c, 0)
     loads[0].wait()
-    maps[s, g] = jnp.concatenate([send_map[...]] * n_slab, axis=1)
-    pl.semaphore_wait(barrier, len(peers))
-
-    def map_copy(to, whose):
+    tiled = jnp.concatenate([send_map[...]] * n_slab, axis=1)
+    lane = iota((n_slab, slots), 1)
+    maps[g, y, z] = jnp.sum(jnp.where(lane // CAP == iota((n_slab, slots), 0), tiled, 0), axis=0, keepdims=True)
+    pl.semaphore_wait(barrier, len(beside) + jnp.minimum(z, 1) + jnp.minimum(deep - 1 - z, 1))
+
+    def hop(block, step):
         return pltpu.make_async_remote_copy(
-            src_ref=maps.at[s, g], dst_ref=maps.at[whose[0], whose[1]],
-            send_sem=map_send.at[to[0], to[1]], recv_sem=map_recv.at[whose[0], whose[1]],
-            device_id=to, device_id_type=MESH)
-
-    for dg, ds in peers:
-        map_copy(peer(dg, ds), (s, g)).start()
-
-    for c in range(chunks // 2, chunks):
-        transform(c, 0)
-
-    for dg, ds in peers:
-        whose = peer(dg, ds)
-        map_copy(whose, whose).wait_recv()
-
-    lane = iota((n_slab, slots), 1)
-    rows = jnp.concatenate(
-        [sum(jnp.where(lane // CAP == a, maps[a, b], 0) for a in range(n_slab)) for b in range(n_grp)],
-        axis=0,
-    )
+            src_ref=maps.at[g, y, block], dst_ref=maps.at[g, y, block],
+            send_sem=hop_send.at[(step + 1) // 2, block], recv_sem=hop_recv.at[block],
+            device_id=(s + 2 * step, g), device_id_type=MESH)
+
+    def for_hops(turn, act):
+        @pl.when((z - turn >= 0) & (z < deep - 1))
+        def _():
+            act(hop(z - turn, 1))
+
+        @pl.when((z + turn <= deep - 1) & (z > 0))
+        def _():
+            act(hop(z + turn, -1))
+
+    def hops_arrive(turn):
+        def arrive(block):
+            pltpu.make_async_remote_copy(
+                src_ref=maps.at[g, y, block], dst_ref=maps.at[g, y, block], send_sem=hop_send.at[0, block],
+                recv_sem=hop_recv.at[block], device_id=beside[0], device_id_type=MESH).wait_recv()
+
+        @pl.when(z - turn >= 0)
+        def _():
+            arrive(z - turn)
+
+        @pl.when(z + turn <= deep - 1)
+        def _():
+            arrive(z + turn)
+
+    for turn in range(deep):
+        if turn > 0:
+            hops_arrive(turn)
+        if turn < deep - 1:
+            for_hops(turn, lambda copy: copy.start())
+        else:
+            over_y = pltpu.make_async_remote_copy(
+                src_ref=maps.at[g, y], dst_ref=maps.at[g, y], send_sem=map_send.at[0],
+                recv_sem=map_recv.at[0], device_id=beside[0], device_id_type=MESH)
+            over_y.start()
+        if turn == 0:
+            loads[1].wait()
+        for c in range(chunks * turn // deep, chunks * (turn + 1) // deep):
+            transform(c, 0)
+    over_y_in = pltpu.make_async_remote_copy(
+        src_ref=maps.at[g, 1 - y], dst_ref=maps.at[g, 1 - y], send_sem=map_send.at[0],
+        recv_sem=map_recv.at[0], device_id=beside[0], device_id_type=MESH)
+    over_y_in.wait_recv()
+
+    def over_grp(to_g, whose_g):
+        return pltpu.make_async_remote_copy(
+            src_ref=maps.at[whose_g], dst_ref=maps.at[whose_g], send_sem=map_send.at[1 + to_g],
+            recv_sem=map_recv.at[1 + whose_g], device_id=(s, to_g), device_id_type=MESH)
+
+    for dg in range(1, n_grp):
+        over_grp(lax.rem(g + dg, n_grp), g).start()
+    for dg in range(1, n_grp):
+        from_g = lax.rem(g + dg, n_grp)
+        over_grp(from_g, from_g).wait_recv()
+
+    def unfold(b):
+        stack = jnp.concatenate(
+            [jnp.where(lane // CAP == iota((n_slab, slots), 0), maps[b, a % 2, a // 2], 0) for a in range(n_slab)],
+            axis=0)
+        for k in (64, 32, 16):
+            stack = stack + pltpu.roll(stack, k, 1)
+        return sum(jnp.where(lane // CAP == a, stack[a * n_slab:(a + 1) * n_slab], 0) for a in range(n_slab))
+
+    rows = jnp.concatenate([unfold(b) for b in range(n_grp)], axis=0)
     shift = ky_loc.bit_length() - 1
     used = rows >= 0
     ky = rows & (NF - 1)
@@ -308,8 +366,7 @@
                     ctf_rows * spec_in[p, :, at:at + 128].astype(jnp.float32)
                 ).astype(jnp.bfloat16)
 
-    own = jnp.sum(jnp.where(lane // CAP == iota((n_slab, slots), 0), maps_row(maps, s, g, n_slab), 0),
-                  axis=0, keepdims=True)
+    own = jnp.sum(jnp.where(iota(rows.shape, 0) == g * n_slab + s, rows, 0), axis=0, keepdims=True)
     own_home = jnp.where(own >= 0, (own & (NF - 1)) >> shift, -1)
     from_a = own_home == iota((n_slab, slots), 0)
     own_rank, ones = ranks(from_a)
@@ -317,8 +374,11 @@
     place = jnp.sum(ones * (own_rank + base + 1.0), axis=0, keepdims=True) - 1.0
     spread = jnp.where(place == iota((n_slab * cap, slots), 0).astype(jnp.float32), 1.0, 0.0).astype(jnp.bfloat16)
 
-    for dg, ds in peers:
-        map_copy(peer(dg, ds), (s, g)).wait_send()
+    for turn in range(deep - 1):
+        for_hops(turn, lambda copy: copy.wait_send())
+    over_y.wait_send()
+    for dg in range(1, n_grp):
+        over_grp(lax.rem(g + dg, n_grp), g).wait_send()
     lane_s = iota((slots, 128), 1)
 
     def lists(half, turn):
@@ -399,10 +459,6 @@
         sum_copy(lax.rem(g + dg, n_grp), g).wait_send()
 
 
-def maps_row(maps, s, g, n_slab):
-    return jnp.concatenate([maps[a, g, pl.ds(s, 1), :] for a in range(n_slab)], axis=0)
-
-
 def run_fused(n_slab, n_grp, cap, collective_id, args):
     pencils, send_map, index, frac, ori_count, spectra, class_ids, ctf = args
     ky_loc, kx_loc = pencils.shape[:2]
@@ -420,7 +476,7 @@
         in_specs=[hbm] * 11,
         out_specs=[vmem, smem],
         scratch_shapes=[
-            pltpu.VMEM((n_slab, n_grp, n_slab, slots), jnp.int32),
+            pltpu.VMEM((n_grp, 2, n_slab // 2, 1, slots), jnp.int32),
             pltpu.VMEM((chunks, 4, kx_loc, 2 * NF), jnp.float32),
             pltpu.VMEM((2 * NF, 2 * NF), jnp.bfloat16),
             pltpu.VMEM((ky_loc // 2, NF, 256), jnp.bfloat16),
@@ -444,8 +500,10 @@
             pltpu.VMEM((ORI_MAX, rows_u), jnp.float32),
             dma((10,)),
             dma((chunks,)),
-            dma((n_slab, n_grp)),
-            dma((n_slab, n_grp)),
+            dma((2, n_slab // 2)),
+            dma((n_slab // 2,)),
+            dma((1 + n_grp,)),
+            dma((1 + n_grp,)),
             dma((n_grp, n_slab)),
             dma((n_grp, n_slab)),
             dma((n_grp,)),

time: 30.7 us -> 35 us (1.14)
  Pallas kernels: 28.1 us -> 32.2 us
    pallas_call x1, Pallas kernels: 28.1 us -> 32.2 us  [run_fused(): pl.pallas_call(lambda *refs: fused(n_slab, n_grp, cap, *refs), out_shape=...]
where the time goes in v4:
time: 35 us; the launch traced here: 34.6 us
  Pallas kernels  32.2 us (92%)
  between operations  1.56 us (4%)
  local copies, waits for them, and re-layouts  0.63 us (2%)
    pallas_call x1, Pallas kernels, run_fused(): pl.pallas_call(lambda *refs: fused(n_slab, n_grp, cap, *refs), out_shape=...  32.2 us

profile of v4, /device:TPU:1, one launch (start us, length us, event | category | flops | bytes accessed | tf_op | source)
XLA Modules:
  0.0 34.6 jit_solution(9127244231700496121)
XLA Ops:
  0.0 0.0 copy-start.4
  0.0 0.0 copy-start.3
  0.0 0.0 copy-start.2
  0.0 0.0 copy-start.1
  0.0 0.0 copy-start.8
  0.0 0.0 copy-start
  0.0 0.0 copy-start.7
  0.0 0.0 copy-start.5
  0.1 0.0 copy-start.6
  0.9 32.2 %shard_map.138 = (f32[8,128]{1,0:T(8,128)S(1)}, s32[1]{0:T(128)}) custom-call(s32[8]{0:T(128)} %refs_0_.1, s32[1]{0:T(128)S(6)} %copy.21.refs_1_, s32[8,16]{1,0:T(8,128)} %bitcast.10, s32[2,8,64]{2,1,0:T(8,128)} %bitcast.8, f32[8,64]{1,0:T(8,128)} %bitcast.12, f32[32,64,512]{2,1,0:T(8,128)} %refs_5_.1, bf16[512,512]{1,0:T(8,128)(2,1)} %constant.9.clone.refs_6_, ...), custom_call_target="tpu_custom_call" | custom-call | tf_op jit(solution)/shard_map/pallas_call | solution.py:470
  33.7 0.0 copy-done.4
  33.7 0.0 copy-done.3
  33.7 0.0 copy-done.2
  33.7 0.0 copy-done.1
  33.7 0.0 copy-done.8
  33.7 0.0 copy-done
  33.7 0.0 copy-done.7
  33.7 0.0 copy-done.5
  33.7 0.0 copy-done.6
  33.8 0.2 conditional.1
  34.0 0.6 %copy.22 = f32[8,128]{1,0:T(8,128)} copy(f32[8,128]{1,0:T(8,128)S(1)} %get-tuple-element.47) | data formatting | bytes 8192
Async XLA Ops:
  0.0 33.7 %copy-start.4 = (f32[256,128]{1,0:T(8,128)S(1)}, f32[256,128]{1,0:T(8,128)}, u32[]{:S(2)}) copy-start(f32[256,128]{1,0:T(8,128)} %constant.11.clone.refs_10_) | copy-start | bytes 393220
  0.0 33.7 %copy-start.3 = (bf16[2,256,256]{2,1,0:T(8,128)(2,1)S(1)}, bf16[2,256,256]{2,1,0:T(8,128)(2,1)}, u32[]{:S(2)}) copy-start(bf16[2,256,256]{2,1,0:T(8,128)(2,1)} %constant.10.clone.refs_9_) | copy-start | bytes 786436
  0.0 33.7 %copy-start.2 = (bf16[512,512]{1,0:T(8,128)(2,1)S(1)}, bf16[512,512]{1,0:T(8,128)(2,1)}, u32[]{:S(2)}) copy-start(bf16[512,512]{1,0:T(8,128)(2,1)} %constant.9.clone.refs_6_) | copy-start | bytes 1572868
  0.0 33.7 %copy-start.1 = (bf16[16,64,256]{2,1,0:T(8,128)(2,1)S(1)}, bf16[16,64,256]{2,1,0:T(8,128)(2,1)}, u32[]{:S(2)}) copy-start(bf16[16,64,256]{2,1,0:T(8,128)(2,1)} %refs_8_.1) | copy-start | bytes 1572868
  0.0 33.7 %copy-start.8 = (s32[8]{0:T(128)S(1)}, s32[8]{0:T(128)}, u32[]{:S(2)}) copy-start(s32[8]{0:T(128)} %refs_0_.1) | copy-start | bytes 100
  0.0 33.7 %copy-start = (bf16[8,64,512]{2,1,0:T(8,128)(2,1)S(1)}, bf16[8,64,512]{2,1,0:T(8,128)(2,1)}, u32[]{:S(2)}) copy-start(bf16[8,64,512]{2,1,0:T(8,128)(2,1)} %refs_7_.1) | copy-start | bytes 1572868
  0.0 33.7 %copy-start.7 = (f32[1,8,64]{2,1,0:T(8,128)S(1)}, f32[1,8,64]{2,1,0:T(8,128)}, u32[]{:S(2)}) copy-start(f32[1,8,64]{2,1,0:T(8,128)} %param.19) | copy-start | bytes 6148
  0.0 33.7 %copy-start.5 = (s32[2,1,8,64]{3,2,1,0:T(8,128)S(1)}, s32[2,1,8,64]{3,2,1,0:T(8,128)}, u32[]{:S(2)}) copy-start(s32[2,1,8,64]{3,2,1,0:T(8,128)} %param.18) | copy-start | bytes 12292
  0.1 33.7 %copy-start.6 = (s32[1,1,8,16]{3,2,1,0:T(8,128)S(1)}, s32[1,1,8,16]{3,2,1,0:T(8,128)}, u32[]{:S(2)}) copy-start(s32[1,1,8,16]{3,2,1,0:T(8,128)} %param.17) | copy-start | bytes 1540

commit v5 on v3

--- a/solution.py
+++ b/solution.py
@@ -151,10 +151,10 @@
 
 def fused(
     n_slab, n_grp, cap,
-    class_hbm, count_hbm, map_hbm, index_hbm, frac_hbm, pencils, dft, spectra, ctf, phase_v, phase_u,
-    out, load_out,
+    class_hbm, map_hbm, index_hbm, frac_hbm, pencils, dft, spectra, ctf, phase_v, phase_u,
+    out, load_out, orient_out,
     maps, lines, table_w, planes, spec_in, ctf_in, col_ph, row_ph, rank_ref, key_ref, picked2, sendbuf,
-    recv, weighted, product, part_send, part_recv, class_ids, ori_count, send_map, index, frac,
+    recv, weighted, product, part_send, part_recv, class_ids, send_map, index, frac,
     load_sem, line_sem, map_send, map_recv, row_send, row_recv, sum_send, sum_recv,
 ):
     s, g = lax.axis_index("slab"), lax.axis_index("grp")
@@ -177,7 +177,7 @@
     loads = [
         pltpu.make_async_copy(a, b, load_sem.at[i])
         for i, (a, b) in enumerate(
-            [(map_hbm, send_map), (dft, table_w), (class_hbm, class_ids), (count_hbm, ori_count),
+            [(map_hbm, send_map), (dft, table_w), (class_hbm, class_ids),
              (index_hbm, index), (frac_hbm, frac), (ctf, ctf_in), (spectra, spec_in), (phase_v, col_ph),
              (phase_u.at[pl.ds(pl.multiple_of(g * rows_u, rows_u), rows_u)], row_ph)]
         )
@@ -205,22 +205,22 @@
         return carry
 
     loads[1].wait()
-    for c in range(chunks // 2):
+    for c in range(chunks // 4):
         transform(c, 0)
     loads[0].wait()
-    maps[s, g] = jnp.concatenate([send_map[...]] * n_slab, axis=1)
+    maps[g, s] = jnp.concatenate([send_map[...]] * n_slab, axis=1)
     pl.semaphore_wait(barrier, len(peers))
 
     def map_copy(to, whose):
         return pltpu.make_async_remote_copy(
-            src_ref=maps.at[s, g], dst_ref=maps.at[whose[0], whose[1]],
+            src_ref=maps.at[g, s], dst_ref=maps.at[whose[1], whose[0]],
             send_sem=map_send.at[to[0], to[1]], recv_sem=map_recv.at[whose[0], whose[1]],
             device_id=to, device_id_type=MESH)
 
     for dg, ds in peers:
         map_copy(peer(dg, ds), (s, g)).start()
 
-    for c in range(chunks // 2, chunks):
+    for c in range(chunks // 4, chunks):
         transform(c, 0)
 
     for dg, ds in peers:
@@ -229,7 +229,7 @@
 
     lane = iota((n_slab, slots), 1)
     rows = jnp.concatenate(
-        [sum(jnp.where(lane // CAP == a, maps[a, b], 0) for a in range(n_slab)) for b in range(n_grp)],
+        [sum(jnp.where(lane // CAP == a, maps[b, a], 0) for a in range(n_slab)) for b in range(n_grp)],
         axis=0,
     )
     shift = ky_loc.bit_length() - 1
@@ -251,11 +251,6 @@
     for b in range(n_grp):
         rank_ref[b] = rank[b * n_slab:(b + 1) * n_slab]
         key_ref[b] = code[b * n_slab:(b + 1) * n_slab]
-    most = jnp.zeros((rows.shape[0], 1), jnp.float32)
-    for a in range(n_slab):
-        most = jnp.maximum(most, jnp.sum(jnp.where(home == a, 1.0, 0.0), axis=1, keepdims=True))
-    load_out[0] = (jnp.max(most) > cap).astype(jnp.int32)
-
     def row_copy(to, whose):
         return pltpu.make_async_remote_copy(
             src_ref=sendbuf.at[to[1], to[0]],
@@ -297,6 +292,11 @@
         pick(i)
     recv[g, pl.ds(pl.multiple_of(s * cap, cap), cap)] = sendbuf[g, s]
 
+    most = jnp.zeros((rows.shape[0], 1), jnp.float32)
+    for a in range(n_slab):
+        most = jnp.maximum(most, jnp.sum(jnp.where(home == a, 1.0, 0.0), axis=1, keepdims=True))
+    load_out[0] = (jnp.max(most) > cap).astype(jnp.int32)
+
     for copy in loads[2:]:
         copy.wait()
     for p in range(PART_DEV):
@@ -340,7 +340,6 @@
             device_id=(s, to_g), device_id_type=MESH)
 
     slot_id = iota((slots, rows_u), 0)
-    live = ori_count[0]
     lane_p = iota((PART_DEV, 128), 1)
 
     def half_score(o, half, received, buf):
@@ -382,7 +381,7 @@
                 else:
                     t = partial[i, e] + t
                     t = (t + pltpu.roll(t, 64, 1)) * (1.0 / NF)
-                    folded.append(jnp.where(o < live, t, 0.0))
+                    folded.append(t)
             if turn == 1:
                 part_send[to_g] = jnp.where(lane_p < 64, folded[0], folded[1])
                 if i < n_grp - 1:
@@ -395,32 +394,34 @@
         sum_copy(from_g, from_g).wait_recv()
         total += part_recv[from_g]
     out[...] = total
+    orient_out[...] = g * (ORI_MAX // n_grp) + lane_p // TRANS
     for dg in range(1, n_grp):
         sum_copy(lax.rem(g + dg, n_grp), g).wait_send()
 
 
 def maps_row(maps, s, g, n_slab):
-    return jnp.concatenate([maps[a, g, pl.ds(s, 1), :] for a in range(n_slab)], axis=0)
+    return jnp.concatenate([maps[g, a, pl.ds(s, 1), :] for a in range(n_slab)], axis=0)
 
 
 def run_fused(n_slab, n_grp, cap, collective_id, args):
-    pencils, send_map, index, frac, ori_count, spectra, class_ids, ctf = args
+    pencils, send_map, index, frac, _, spectra, class_ids, ctf = args
     ky_loc, kx_loc = pencils.shape[:2]
     rows_u = spectra.shape[1]
     slots = n_slab * CAP
     chunks = ky_loc // 4
-    vmem, smem, hbm = (pl.BlockSpec(memory_space=m) for m in (pltpu.VMEM, pltpu.SMEM, pl.ANY))
+    vmem, smem = (pl.BlockSpec(memory_space=m) for m in (pltpu.VMEM, pltpu.SMEM))
     dma = pltpu.SemaphoreType.DMA
     return pl.pallas_call(
         lambda *refs: fused(n_slab, n_grp, cap, *refs),
         out_shape=[
             jax.ShapeDtypeStruct((PART_DEV, ORI_MAX * TRANS // n_grp), jnp.float32),
             jax.ShapeDtypeStruct((1,), jnp.int32),
+            jax.ShapeDtypeStruct((PART_DEV, ORI_MAX * TRANS // n_grp), jnp.int32),
         ],
-        in_specs=[hbm] * 11,
-        out_specs=[vmem, smem],
+        in_specs=[pl.BlockSpec(memory_space=pltpu.HBM)] * 10,
+        out_specs=[vmem, smem, vmem],
         scratch_shapes=[
-            pltpu.VMEM((n_slab, n_grp, n_slab, slots), jnp.int32),
+            pltpu.VMEM((n_grp, n_slab, n_slab, slots), jnp.int32),
             pltpu.VMEM((chunks, 4, kx_loc, 2 * NF), jnp.float32),
             pltpu.VMEM((2 * NF, 2 * NF), jnp.bfloat16),
             pltpu.VMEM((ky_loc // 2, NF, 256), jnp.bfloat16),
@@ -438,11 +439,10 @@
             pltpu.VMEM((n_grp, PART_DEV, 128), jnp.float32),
             pltpu.VMEM((n_grp, PART_DEV, 128), jnp.float32),
             pltpu.SMEM(class_ids.shape, jnp.int32),
-            pltpu.SMEM(ori_count.shape, jnp.int32),
             pltpu.VMEM(send_map.shape[2:], jnp.int32),
             pltpu.VMEM((2, ORI_MAX, rows_u), jnp.int32),
             pltpu.VMEM((ORI_MAX, rows_u), jnp.float32),
-            dma((10,)),
+            dma((9,)),
             dma((chunks,)),
             dma((n_slab, n_grp)),
             dma((n_slab, n_grp)),
@@ -454,18 +454,19 @@
         compiler_params=pltpu.CompilerParams(
             collective_id=collective_id, has_side_effects=True, vmem_limit_bytes=60 * 2**20),
     )(
-        class_ids, ori_count, send_map[0, 0], index[:, 0], frac[0], pencils, jnp.asarray(dft_table()),
+        class_ids, send_map[0, 0], index[:, 0], frac[0], pencils, jnp.asarray(dft_table()),
         spectra, ctf, jnp.asarray(column_phases()), jnp.asarray(row_phases()),
     )
 
 
 def listed(n_slab, n_grp, *args):
-    scores, load = run_fused(n_slab, n_grp, CAP_FAST, 1, args)
-    return lax.cond(
+    scores, load, orient = run_fused(n_slab, n_grp, CAP_FAST, 1, args)
+    chosen = lax.cond(
         load.reshape(()) > 0,
         lambda: run_fused(n_slab, n_grp, n_slab * CAP, 2, args)[0],
         lambda: scores,
     )
+    return jnp.where(orient < args[4][0], chosen, 0.0)
 
 
 def solution(mesh):

time: 30.7 us -> 30.6 us (level)
  other arithmetic: 0 us -> 0.6 us
  local copies, waits for them, and re-layouts: 0.63 us -> 0.04 us
    select_n x0 -> x1, other arithmetic: none -> 0.6 us  [listed(): return jnp.where(orient < args[4][0], chosen, 0.0)]
    unnamed x19 -> x20, local copies, waits for them, and re-layouts: 0.63 us -> 0.04 us
where the time goes in v5:
time: 30.6 us; the launch traced here: 30.5 us
  Pallas kernels  28.2 us (92%)
  between operations  1.43 us (5%)
  other arithmetic  0.6 us (2%)
    pallas_call x1, Pallas kernels, run_fused(): pl.pallas_call(lambda *refs: fused(n_slab, n_grp, cap, *refs), out_shape=...  28.2 us

profile of v5, /device:TPU:1, one launch (start us, length us, event | category | flops | bytes accessed | tf_op | source)
XLA Modules:
  0.0 30.5 jit_solution(1910436686491493310)
XLA Ops:
  0.0 0.0 copy-start.2
  0.0 0.0 copy-start.3
  0.0 0.0 copy-start.4
  0.0 0.0 copy-start.6
  0.0 0.0 copy-start.5
  0.0 0.0 copy-start.7
  0.0 0.0 copy-start
  0.0 0.0 copy-start.9
  0.1 0.0 copy-start.1
  0.1 28.2 %shard_map.136 = (f32[8,128]{1,0:T(8,128)S(1)}, s32[1]{0:T(128)}, s32[8,128]{1,0:T(8,128)}) custom-call(s32[8]{0:T(128)} %refs_0_.1, s32[8,16]{1,0:T(8,128)} %bitcast.12, s32[2,8,64]{2,1,0:T(8,128)} %bitcast.10, f32[8,64]{1,0:T(8,128)} %bitcast.14, f32[32,64,512]{2,1,0:T(8,128)} %refs_4_.1, bf16[512,512]{1,0:T(8,128)(2,1)} %constant.11.clone.refs_5_, ...), custom_call_target="tpu_custom_call" | custom-call | tf_op jit(solution)/shard_map/pallas_call | solution.py:414
  28.3 0.0 copy-start.8
  28.9 0.0 copy-done.2
  28.9 0.0 copy-done.3
  28.9 0.0 copy-done.4
  28.9 0.0 copy-done.6
  28.9 0.0 copy-done.5
  28.9 0.0 copy-done.7
  29.0 0.0 copy-done
  29.0 0.0 copy-done.9
  29.0 0.0 copy-done.1
  29.0 0.2 conditional.1
  29.9 0.0 copy-done.8
  29.9 0.6 %compare_select_fusion = f32[8,128]{1,0:T(8,128)} fusion(f32[8,128]{1,0:T(8,128)S(1)} %get-tuple-element.56, s32[8,128]{1,0:T(8,128)S(1)} %copy-done.8, s32[]{:T(128)} %bitcast.9), kind=kLoop, calls=%fused_computation | loop fusion | flops 2048 | bytes 12292 | tf_op jit(solution)/shard_map/jit(_where)/select_n | solution.py:469
Async XLA Ops:
  0.0 28.9 %copy-start.2 = (bf16[512,512]{1,0:T(8,128)(2,1)S(1)}, bf16[512,512]{1,0:T(8,128)(2,1)}, u32[]{:S(2)}) copy-start(bf16[512,512]{1,0:T(8,128)(2,1)} %constant.11.clone.refs_5_) | copy-start | bytes 1572868
  0.0 28.9 %copy-start.3 = (bf16[2,256,256]{2,1,0:T(8,128)(2,1)S(1)}, bf16[2,256,256]{2,1,0:T(8,128)(2,1)}, u32[]{:S(2)}) copy-start(bf16[2,256,256]{2,1,0:T(8,128)(2,1)} %constant.12.clone.refs_8_) | copy-start | bytes 786436
  0.0 28.9 %copy-start.4 = (f32[256,128]{1,0:T(8,128)S(1)}, f32[256,128]{1,0:T(8,128)}, u32[]{:S(2)}) copy-start(f32[256,128]{1,0:T(8,128)} %constant.13.clone.refs_9_) | copy-start | bytes 393220
  0.0 28.9 %copy-start.6 = (s32[1,1,8,16]{3,2,1,0:T(8,128)S(1)}, s32[1,1,8,16]{3,2,1,0:T(8,128)}, u32[]{:S(2)}) copy-start(s32[1,1,8,16]{3,2,1,0:T(8,128)} %param.17) | copy-start | bytes 1540
  0.0 28.9 %copy-start.5 = (s32[2,1,8,64]{3,2,1,0:T(8,128)S(1)}, s32[2,1,8,64]{3,2,1,0:T(8,128)}, u32[]{:S(2)}) copy-start(s32[2,1,8,64]{3,2,1,0:T(8,128)} %param.18) | copy-start | bytes 12292
  0.0 28.9 %copy-start.7 = (f32[1,8,64]{2,1,0:T(8,128)S(1)}, f32[1,8,64]{2,1,0:T(8,128)}, u32[]{:S(2)}) copy-start(f32[1,8,64]{2,1,0:T(8,128)} %param.19) | copy-start | bytes 6148
  0.0 28.9 %copy-start = (bf16[8,64,512]{2,1,0:T(8,128)(2,1)S(1)}, bf16[8,64,512]{2,1,0:T(8,128)(2,1)}, u32[]{:S(2)}) copy-start(bf16[8,64,512]{2,1,0:T(8,128)(2,1)} %refs_6_.1) | copy-start | bytes 1572868
  0.0 28.9 %copy-start.9 = (s32[8]{0:T(128)S(1)}, s32[8]{0:T(128)}, u32[]{:S(2)}) copy-start(s32[8]{0:T(128)} %refs_0_.1) | copy-start | bytes 100
  0.1 28.9 %copy-start.1 = (bf16[16,64,256]{2,1,0:T(8,128)(2,1)S(1)}, bf16[16,64,256]{2,1,0:T(8,128)(2,1)}, u32[]{:S(2)}) copy-start(bf16[16,64,256]{2,1,0:T(8,128)(2,1)} %refs_7_.1) | copy-start | bytes 1572868
  28.3 1.6 %copy-start.8 = (s32[8,128]{1,0:T(8,128)S(1)}, s32[8,128]{1,0:T(8,128)}, u32[]{:S(2)}) copy-start(s32[8,128]{1,0:T(8,128)} %get-tuple-element.43) | copy-start | bytes 12292

commit v6 on v5

--- a/solution.py
+++ b/solution.py
@@ -151,10 +151,10 @@
 
 def fused(
     n_slab, n_grp, cap,
-    class_hbm, map_hbm, index_hbm, frac_hbm, pencils, dft, spectra, ctf, phase_v, phase_u,
-    out, load_out, orient_out,
+    class_hbm, count_hbm, map_hbm, index_hbm, frac_hbm, pencils, dft, spectra, ctf, phase_v, phase_u,
+    out, load_out, listed_out,
     maps, lines, table_w, planes, spec_in, ctf_in, col_ph, row_ph, rank_ref, key_ref, picked2, sendbuf,
-    recv, weighted, product, part_send, part_recv, class_ids, send_map, index, frac,
+    recv, weighted, product, part_send, part_recv, class_ids, ori_count, send_map, index, frac,
     load_sem, line_sem, map_send, map_recv, row_send, row_recv, sum_send, sum_recv,
 ):
     s, g = lax.axis_index("slab"), lax.axis_index("grp")
@@ -177,7 +177,7 @@
     loads = [
         pltpu.make_async_copy(a, b, load_sem.at[i])
         for i, (a, b) in enumerate(
-            [(map_hbm, send_map), (dft, table_w), (class_hbm, class_ids),
+            [(map_hbm, send_map), (dft, table_w), (class_hbm, class_ids), (count_hbm, ori_count),
              (index_hbm, index), (frac_hbm, frac), (ctf, ctf_in), (spectra, spec_in), (phase_v, col_ph),
              (phase_u.at[pl.ds(pl.multiple_of(g * rows_u, rows_u), rows_u)], row_ph)]
         )
@@ -394,7 +394,7 @@
         sum_copy(from_g, from_g).wait_recv()
         total += part_recv[from_g]
     out[...] = total
-    orient_out[...] = g * (ORI_MAX // n_grp) + lane_p // TRANS
+    listed_out[...] = jnp.where(g * (ORI_MAX // n_grp) + lane_p // TRANS < ori_count[...], 1, 0)
     for dg in range(1, n_grp):
         sum_copy(lax.rem(g + dg, n_grp), g).wait_send()
 
@@ -404,7 +404,7 @@
 
 
 def run_fused(n_slab, n_grp, cap, collective_id, args):
-    pencils, send_map, index, frac, _, spectra, class_ids, ctf = args
+    pencils, send_map, index, frac, count, spectra, class_ids, ctf = args
     ky_loc, kx_loc = pencils.shape[:2]
     rows_u = spectra.shape[1]
     slots = n_slab * CAP
@@ -418,7 +418,7 @@
             jax.ShapeDtypeStruct((1,), jnp.int32),
             jax.ShapeDtypeStruct((PART_DEV, ORI_MAX * TRANS // n_grp), jnp.int32),
         ],
-        in_specs=[pl.BlockSpec(memory_space=pltpu.HBM)] * 10,
+        in_specs=[pl.BlockSpec(memory_space=pltpu.HBM)] * 11,
         out_specs=[vmem, smem, vmem],
         scratch_shapes=[
             pltpu.VMEM((n_grp, n_slab, n_slab, slots), jnp.int32),
@@ -439,10 +439,11 @@
             pltpu.VMEM((n_grp, PART_DEV, 128), jnp.float32),
             pltpu.VMEM((n_grp, PART_DEV, 128), jnp.float32),
             pltpu.SMEM(class_ids.shape, jnp.int32),
+            pltpu.VMEM((1, 1), jnp.int32),
             pltpu.VMEM(send_map.shape[2:], jnp.int32),
             pltpu.VMEM((2, ORI_MAX, rows_u), jnp.int32),
             pltpu.VMEM((ORI_MAX, rows_u), jnp.float32),
-            dma((9,)),
+            dma((10,)),
             dma((chunks,)),
             dma((n_slab, n_grp)),
             dma((n_slab, n_grp)),
@@ -454,19 +455,20 @@
         compiler_params=pltpu.CompilerParams(
             collective_id=collective_id, has_side_effects=True, vmem_limit_bytes=60 * 2**20),
     )(
-        class_ids, send_map[0, 0], index[:, 0], frac[0], pencils, jnp.asarray(dft_table()),
+        class_ids, count.reshape(1, 1), send_map[0, 0], index[:, 0], frac[0], pencils, jnp.asarray(dft_table()),
         spectra, ctf, jnp.asarray(column_phases()), jnp.asarray(row_phases()),
     )
 
 
 def listed(n_slab, n_grp, *args):
-    scores, load, orient = run_fused(n_slab, n_grp, CAP_FAST, 1, args)
+    scores, load, in_list = run_fused(n_slab, n_grp, CAP_FAST, 1, args)
+    any_list = (*args[:4], jnp.zeros((1,), jnp.int32), *args[5:])
     chosen = lax.cond(
         load.reshape(()) > 0,
-        lambda: run_fused(n_slab, n_grp, n_slab * CAP, 2, args)[0],
+        lambda: run_fused(n_slab, n_grp, n_slab * CAP, 2, any_list)[0],
         lambda: scores,
     )
-    return jnp.where(orient < args[4][0], chosen, 0.0)
+    return jnp.where(in_list > 0, chosen, 0.0)
 
 
 def solution(mesh):

time: 30.6 us -> 30.8 us (level)
  no operation moved by 1% of the time
where the time goes in v6:
time: 30.8 us; the launch traced here: 30.7 us
  Pallas kernels  28.3 us (92%)
  between operations  1.57 us (5%)
  other arithmetic  0.6 us (2%)
    pallas_call x1, Pallas kernels, run_fused(): pl.pallas_call(lambda *refs: fused(n_slab, n_grp, cap, *refs), out_shape=...  28.3 us

profile of v6, /device:TPU:1, one launch (start us, length us, event | category | flops | bytes accessed | tf_op | source)
XLA Modules:
  0.0 30.7 jit_solution(13105954571693931163)
XLA Ops:
  0.0 0.0 copy-start.4
  0.0 0.0 copy-start.3
  0.0 0.0 copy-start.2
  0.0 0.0 copy-start.1
  0.0 0.0 copy-start.9
  0.0 0.0 copy-start
  0.0 0.0 copy-start.7
  0.0 0.0 copy-start.5
  0.1 0.0 copy-start.6
  0.8 28.3 %shard_map.136 = (f32[8,128]{1,0:T(8,128)S(1)}, s32[1]{0:T(128)}, s32[8,128]{1,0:T(8,128)}) custom-call(s32[8]{0:T(128)} %refs_0_.1, s32[1,1]{1,0:T(1,128)} %bitcast.9.refs_1_, s32[8,16]{1,0:T(8,128)} %bitcast.12, s32[2,8,64]{2,1,0:T(8,128)} %bitcast.10, f32[8,64]{1,0:T(8,128)} %bitcast.14, f32[32,64,512]{2,1,0:T(8,128)} %refs_5_.1, ...), custom_call_target="tpu_custom_call" | custom-call | tf_op jit(solution)/shard_map/pallas_call | solution.py:414
  29.1 0.0 copy-start.8
  29.8 0.0 copy-done.4
  29.8 0.0 copy-done.3
  29.8 0.0 copy-done.2
  29.8 0.0 copy-done.1
  29.8 0.0 copy-done.9
  29.8 0.0 copy-done
  29.8 0.0 copy-done.7
  29.8 0.0 copy-done.5
  29.8 0.0 copy-done.6
  29.8 0.2 conditional.1
  30.1 0.0 copy-done.8
  30.1 0.6 %compare_select_fusion = f32[8,128]{1,0:T(8,128)} fusion(f32[8,128]{1,0:T(8,128)S(1)} %get-tuple-element.56, s32[8,128]{1,0:T(8,128)S(1)} %copy-done.8), kind=kLoop, calls=%fused_computation | loop fusion | flops 2048 | bytes 12288 | tf_op jit(solution)/shard_map/jit(_where)/select_n | solution.py:471
Async XLA Ops:
  0.0 29.8 %copy-start.4 = (f32[256,128]{1,0:T(8,128)S(1)}, f32[256,128]{1,0:T(8,128)}, u32[]{:S(2)}) copy-start(f32[256,128]{1,0:T(8,128)} %constant.17.clone.refs_10_) | copy-start | bytes 393220
  0.0 29.8 %copy-start.3 = (bf16[2,256,256]{2,1,0:T(8,128)(2,1)S(1)}, bf16[2,256,256]{2,1,0:T(8,128)(2,1)}, u32[]{:S(2)}) copy-start(bf16[2,256,256]{2,1,0:T(8,128)(2,1)} %constant.16.clone.refs_9_) | copy-start | bytes 786436
  0.0 29.8 %copy-start.2 = (bf16[512,512]{1,0:T(8,128)(2,1)S(1)}, bf16[512,512]{1,0:T(8,128)(2,1)}, u32[]{:S(2)}) copy-start(bf16[512,512]{1,0:T(8,128)(2,1)} %constant.15.clone.refs_6_) | copy-start | bytes 1572868
  0.0 29.8 %copy-start.1 = (bf16[16,64,256]{2,1,0:T(8,128)(2,1)S(1)}, bf16[16,64,256]{2,1,0:T(8,128)(2,1)}, u32[]{:S(2)}) copy-start(bf16[16,64,256]{2,1,0:T(8,128)(2,1)} %refs_8_.1) | copy-start | bytes 1572868
  0.0 29.8 %copy-start.9 = (s32[8]{0:T(128)S(1)}, s32[8]{0:T(128)}, u32[]{:S(2)}) copy-start(s32[8]{0:T(128)} %refs_0_.1) | copy-start | bytes 100
  0.0 29.8 %copy-start = (bf16[8,64,512]{2,1,0:T(8,128)(2,1)S(1)}, bf16[8,64,512]{2,1,0:T(8,128)(2,1)}, u32[]{:S(2)}) copy-start(bf16[8,64,512]{2,1,0:T(8,128)(2,1)} %refs_7_.1) | copy-start | bytes 1572868
  0.0 29.8 %copy-start.7 = (f32[1,8,64]{2,1,0:T(8,128)S(1)}, f32[1,8,64]{2,1,0:T(8,128)}, u32[]{:S(2)}) copy-start(f32[1,8,64]{2,1,0:T(8,128)} %param.19) | copy-start | bytes 6148
  0.0 29.8 %copy-start.5 = (s32[2,1,8,64]{3,2,1,0:T(8,128)S(1)}, s32[2,1,8,64]{3,2,1,0:T(8,128)}, u32[]{:S(2)}) copy-start(s32[2,1,8,64]{3,2,1,0:T(8,128)} %param.18) | copy-start | bytes 12292
  0.1 29.8 %copy-start.6 = (s32[1,1,8,16]{3,2,1,0:T(8,128)S(1)}, s32[1,1,8,16]{3,2,1,0:T(8,128)}, u32[]{:S(2)}) copy-start(s32[1,1,8,16]{3,2,1,0:T(8,128)} %param.17) | copy-start | bytes 1540
  29.1 1.0 %copy-start.8 = (s32[8,128]{1,0:T(8,128)S(1)}, s32[8,128]{1,0:T(8,128)}, u32[]{:S(2)}) copy-start(s32[8,128]{1,0:T(8,128)} %get-tuple-element.43) | copy-start | bytes 12292
